TPU v7x, 32 devices: a whole 2x2x4 slice. The times are simulated.
32 devices in a mesh: seq: 8 (over y, x, core), tp: 4 (over z).
Axes of the slice: x: 2, y: 2, z: 4, core: 2. Of those that a mesh axis runs over, the one named last changes fastest.
Arguments:
- byte_ids: int32 [1024, 8], P('seq'), may hold values from 0 to 255
- global_out: bfloat16 [1024, 8192], P('seq', 'tp'), may hold values from -6 to 6
- global_in_grad: bfloat16 [1024, 8192], P('seq', 'tp'), may hold values from -6 to 6
- out_grad: bfloat16 [8192, 1024], P(('seq', 'tp')), may hold values from -6 to 6
- proj_weight: bfloat16 [1024, 1024], replicated, may hold values from -0.1875 to 0.1875
- emb_local: bfloat16 [256, 1024], replicated, may hold values from -6 to 6
- norm_gain: float32 [1024], replicated, may hold values from 0.1 to 1.9
- up_weight: bfloat16 [1024, 2048], replicated, may hold values from -0.1875 to 0.1875
- down_weight: bfloat16 [2048, 1024], replicated, may hold values from -0.125 to 0.125
Outputs:
- glob_out_grad: bfloat16 [1024, 8192], P('seq', 'tp')
- emb_global_grad: float32 [256, 1024], replicated
- emb_local_grad: float32 [256, 1024], replicated
- gain_grad: float32 [1024], replicated
- proj_grad: float32 [1024, 1024], P(None, ('seq', 'tp'))
- up_grad: float32 [1024, 2048], P(None, ('seq', 'tp'))
- down_grad: float32 [2048, 1024], P(('seq', 'tp'))
All inputs are finite; a program needn't handle non-finite values.
Results may differ from a plain program's by a relative error of at most 0.015.
Values may be sent and summed in bfloat16 or wider, within the bound.
No kernel may reach another device: no remote copies, remote signals or barrier semaphores. Data moves between devices by JAX's collectives and lax.ppermute only.
A program may use at most 128 MiB of HBM per device.

v0:
```python
import jax
import jax.numpy as jnp
from jax import lax
from jax.sharding import PartitionSpec as P


def inner(left, right):
    return lax.dot_general(
        left, right, (((0,), (0,)), ((), ())), preferred_element_type=jnp.float32
    )


def outer(left, right):
    return lax.dot_general(
        left, right, (((1,), (1,)), ((), ())), preferred_element_type=jnp.float32
    )


def on_device(
    byte_ids,
    global_out,
    global_in_grad,
    out_grad,
    proj_weight,
    emb_local,
    norm_gain,
    up_weight,
    down_weight,
):
    tp_count = lax.axis_size("tp")
    tp_place = lax.axis_index("tp")
    patch = byte_ids.shape[1]
    slot = proj_weight.shape[0]
    vocab = emb_local.shape[0]
    local_patches = global_out.shape[0] // tp_count
    local_ids = lax.dynamic_slice_in_dim(byte_ids, tp_place * local_patches, local_patches, 0)
    local_out = lax.all_to_all(global_out, "tp", split_axis=0, concat_axis=1, tiled=True)
    slot_in = local_out.reshape(local_patches * patch, slot)
    first = jnp.full((local_patches, 1), -1, jnp.int32)
    prev_id = jnp.concatenate([first, local_ids[:, :-1]], axis=1).reshape(-1)
    prev_hot = jax.nn.one_hot(prev_id, vocab, dtype=jnp.bfloat16)
    u_rows = jnp.dot(slot_in, proj_weight, preferred_element_type=jnp.float32) + jnp.dot(
        prev_hot, emb_local, preferred_element_type=jnp.float32
    )
    scale = lax.rsqrt(jnp.mean(u_rows * u_rows, axis=1, keepdims=True) + 1e-05)
    normed = u_rows * scale
    r_rows = (normed * norm_gain).astype(jnp.bfloat16)
    a_rows = jnp.dot(r_rows, up_weight, preferred_element_type=jnp.float32)
    sig = jax.nn.sigmoid(a_rows)
    h_rows = (a_rows * sig).astype(jnp.bfloat16)
    dh_rows = outer(out_grad, down_weight)
    da_rows = (dh_rows * sig * (1.0 + a_rows * (1.0 - sig))).astype(jnp.bfloat16)
    dr_rows = outer(da_rows, up_weight)
    dn_rows = dr_rows * norm_gain
    du_rows = (
        out_grad.astype(jnp.float32)
        + scale * (dn_rows - normed * jnp.mean(dn_rows * normed, axis=1, keepdims=True))
    ).astype(jnp.bfloat16)
    local_back = (
        outer(du_rows, proj_weight).astype(jnp.bfloat16).reshape(local_patches, patch * slot)
    )
    glob_out_grad = lax.all_to_all(local_back, "tp", split_axis=1, concat_axis=0, tiled=True)
    slots_here = patch // tp_count
    own_ids = lax.dynamic_slice_in_dim(byte_ids, tp_place * slots_here, slots_here, 1).reshape(-1)
    own_hot = jax.nn.one_hot(own_ids, vocab, dtype=jnp.bfloat16)
    emb_global_part = inner(own_hot, global_in_grad.reshape(-1, slot))
    emb_local_part = inner(prev_hot, du_rows)
    gain_part = jnp.sum(dr_rows * normed, axis=0)
    emb_global_grad, emb_local_grad, gain_grad = lax.psum(
        (emb_global_part, emb_local_part, gain_part), ("seq", "tp")
    )
    proj_part = inner(slot_in, du_rows)
    up_part = inner(r_rows, da_rows)
    down_part = inner(h_rows, out_grad)
    proj_half, up_half, down_half = (
        lax.psum_scatter(
            proj_part.astype(jnp.bfloat16), "seq", scatter_dimension=1, tiled=True
        ).astype(jnp.float32),
        lax.psum_scatter(
            up_part.astype(jnp.bfloat16), "seq", scatter_dimension=1, tiled=True
        ).astype(jnp.float32),
        lax.psum_scatter(
            down_part.astype(jnp.bfloat16), "seq", scatter_dimension=0, tiled=True
        ).astype(jnp.float32),
    )
    proj_grad, up_grad, down_grad = (
        lax.psum_scatter(
            proj_half.astype(jnp.bfloat16), "tp", scatter_dimension=1, tiled=True
        ).astype(jnp.float32),
        lax.psum_scatter(
            up_half.astype(jnp.bfloat16), "tp", scatter_dimension=1, tiled=True
        ).astype(jnp.float32),
        lax.psum_scatter(
            down_half.astype(jnp.bfloat16), "tp", scatter_dimension=0, tiled=True
        ).astype(jnp.float32),
    )
    return (
        glob_out_grad,
        emb_global_grad,
        emb_local_grad,
        gain_grad,
        proj_grad,
        up_grad,
        down_grad,
    )


def solution(mesh):
    placed = (
        P("seq", None),
        P("seq", "tp"),
        P("seq", "tp"),
        P(("seq", "tp"), None),
        P(),
        P(),
        P(),
        P(),
        P(),
    )
    return jax.shard_map(
        on_device,
        mesh=mesh,
        in_specs=placed,
        out_specs=(
            P("seq", "tp"),
            P(),
            P(),
            P(),
            P(None, ("seq", "tp")),
            P(None, ("seq", "tp")),
            P(("seq", "tp"), None),
        ),
        check_vma=False,
    )
```

profile of v0, /device:TPU:0, one launch (start us, length us, event | category | flops | bytes accessed | tf_op | source)
XLA Modules:
  0.0 357.2 jit_solution(3450945052802741419)
XLA Ops:
  8.0 6.5 %all-to-all-start = ((bf16[4,32,2048]{2,1,0:T(8,128)(2,1)}), bf16[4,32,2048]{2,1,0:T(8,128)(2,1)S(1)}, u32[]{:S(2)}, u32[]{:S(2)}) async-start(bf16[4,32,2048]{2,1,0:T(8,128)(2,1)} %bitcast.29), calls=%async_computation | async-start | bytes 1048576 | tf_op jit(solution)/shard_map/all_to_all | solution.py:37
  15.5 13.5 %all-to-all-done = bf16[4,32,2048]{2,1,0:T(8,128)(2,1)S(1)} async-done(((bf16[4,32,2048]{2,1,0:T(8,128)(2,1)}), bf16[4,32,2048]{2,1,0:T(8,128)(2,1)S(1)}, u32[]{:S(2)}, u32[]{:S(2)}) %all-to-all-start) | async-done | bytes 524320 | tf_op jit(solution)/shard_map/all_to_all | solution.py:37
  29.5 0.8 copy-done.1
  31.0 1.8 multiply_reduce_fusion.2
  32.9 1.3 fusion.9
  34.2 1.0 copy-done.12
  35.2 1.5 fusion.1
  36.8 1.5 multiply_reduce_fusion
  38.7 0.8 copy-done.3
  39.5 2.1 convert_bitcast_fusion
  41.6 4.6 %convolution_convert_fusion.1 = bf16[1024,2048]{1,0:T(8,128)(2,1)} fusion(bf16[256,2048]{1,0:T(8,128)(2,1)} %copy-done.7, f32[256,1024]{1,0:T(8,128)S(1)} %get-tuple-element.33, f32[1024]{0:T(1024)S(1)} %copy-done.11, f32[256]{0:T(256)S(1)} %add_rsqrt_fusion), kind=kOutput, calls=%fused_computation.1 | convolution fusion | flops 1076625408 | bytes 6296576 | tf_op jit(solution)/shard_map/dot_general | solution.py:8
  46.3 1.0 copy-done.10
  47.3 5.0 %convolution_convert_fusion = bf16[2048,1024]{1,0:T(8,128)(2,1)} fusion(bf16[256,1024]{1,0:T(8,128)(2,1)S(1)} %copy-done.10, f32[256,2048]{1,0:T(8,128)} %copy-done.6), kind=kOutput, calls=%fused_computation | convolution fusion | flops 1078460416 | bytes 6815744 | tf_op jit(solution)/shard_map/dot_general | solution.py:8
  52.4 29.7 %reduce-scatter.9.cloned.1.call-done = bf16[1024,128]{0,1:T(8,128)(2,1)} async-done(((bf16[1024,1024]{0,1:T(8,128)(2,1)}), bf16[1024,128]{0,1:T(8,128)(2,1)}) %reduce-scatter.9.cloned.1.call-update) | async-done | bytes 262160 | tf_op jit(solution)/shard_map/reduce_scatter | solution.py:76
  82.2 54.6 %reduce-scatter.13.cloned.1.call-done = bf16[1024,256]{1,0:T(8,128)(2,1)} async-done(((bf16[1024,2048]{1,0:T(8,128)(2,1)}), bf16[1024,256]{1,0:T(8,128)(2,1)}) %reduce-scatter.13.cloned.1.call-update) | async-done | bytes 524304 | tf_op jit(solution)/shard_map/reduce_scatter | solution.py:79
  136.8 2.1 copy.28
  139.0 53.0 %reduce-scatter.15.cloned.1.call-done = bf16[256,1024]{1,0:T(8,128)(2,1)} async-done(((bf16[2048,1024]{1,0:T(8,128)(2,1)}), bf16[256,1024]{1,0:T(8,128)(2,1)}) %reduce-scatter.15.cloned.1.call-update) | async-done | bytes 524304 | tf_op jit(solution)/shard_map/reduce_scatter | solution.py:82
  193.1 1.2 reshape.49
  194.4 1.4 fusion.4
  195.8 1.4 fusion.3
  198.3 1.1 copy.25
  199.4 4.6 %all-to-all-start.1 = ((bf16[32,4,2048]{2,0,1:T(8,128)(2,1)}), bf16[32,4,2048]{2,0,1:T(8,128)(2,1)S(1)}, u32[]{:S(2)}, u32[]{:S(2)}) async-start(bf16[32,4,2048]{2,0,1:T(8,128)(2,1)} %copy.25), calls=%async_computation.1 | async-start | bytes 1048576 | tf_op jit(solution)/shard_map/all_to_all | solution.py:62
  204.0 41.2 %psum.23 = f32[1024]{0:T(1024)} all-reduce(f32[1024]{0:T(1024)S(1)} %get-tuple-element.28), channel_id=1, replica_groups=mesh['seq'=8,'tp'=4] {'seq','tp'}, use_global_device_ids=true, to_apply=%region_5.6 | all-reduce | flops 1024 | bytes 8192 | tf_op jit(solution)/shard_map/psum | solution.py:69
  245.2 1.5 convert_element_type.55
  246.8 1.1 copy.29
  247.8 0.8 copy.27
  248.7 19.7 %reduce-scatter.17.cloned.1.call-done = bf16[64,1024]{1,0:T(8,128)(2,1)} async-done(((bf16[256,1024]{1,0:T(8,128)(2,1)}), bf16[64,1024]{1,0:T(8,128)(2,1)}) %reduce-scatter.17.cloned.1.call-update) | async-done | bytes 131088 | tf_op jit(solution)/shard_map/reduce_scatter | solution.py:93
  268.3 1.6 convert_element_type.60
  270.0 75.7 %all-reduce.4.cloned.1.call-done = (f32[256,1024]{1,0:T(8,128)}, f32[256,1024]{1,0:T(8,128)}) async-done(((f32[256,1024]{1,0:T(8,128)}, f32[256,1024]{1,0:T(8,128)}), (f32[256,1024]{1,0:T(8,128)}, f32[256,1024]{1,0:T(8,128)})) %all-reduce.4.cloned.1.call-update) | async-done | bytes 2097168 | tf_op jit(solution)/shard_map/psum | solution.py:69
  345.7 0.8 copy.34
  346.4 2.3 copy.35
  348.8 1.0 copy.36
  (54 shorter events, 5.3 us)
Async XLA Ops:
  8.0 22.3 %copy-start = (bf16[1024,1024]{1,0:T(8,128)(2,1)S(1)}, bf16[1024,1024]{1,0:T(8,128)(2,1)}, u32[]{:S(2)}) copy-start(bf16[1024,1024]{1,0:T(8,128)(2,1)} %param.13) | copy-start | bytes 6291460
  8.0 21.0 %all-to-all-start = ((bf16[4,32,2048]{2,1,0:T(8,128)(2,1)}), bf16[4,32,2048]{2,1,0:T(8,128)(2,1)S(1)}, u32[]{:S(2)}, u32[]{:S(2)}) async-start(bf16[4,32,2048]{2,1,0:T(8,128)(2,1)} %bitcast.29), calls=%async_computation | async-start | bytes 1048576 | tf_op jit(solution)/shard_map/all_to_all | solution.py:37
  14.5 67.6 %reduce-scatter.9.cloned.1.call-start = ((), (), s32[]{:S(2)}) async-start(), calls=%async_computation.8 | async-start | bytes 2359296 | tf_op jit(solution)/shard_map/reduce_scatter | solution.py:76
  29.5 0.8 copy-start.1
  30.3 2.6 copy-start.5
  31.0 1.9 copy-start.11
  32.9 1.3 copy-start.9
  32.9 2.4 copy-start.12
  35.2 1.6 copy-start.6
  36.8 1.5 copy-start.7
  38.3 1.1 copy-start.2
  38.7 0.8 copy-start.3
  41.6 95.2 %reduce-scatter.13.cloned.1.call-start = ((), (), s32[]{:S(2)}) async-start(), calls=%async_computation.10 | async-start | bytes 4718592 | tf_op jit(solution)/shard_map/reduce_scatter | solution.py:79
  46.2 1.0 copy-start.10
  46.2 145.7 %reduce-scatter.15.cloned.1.call-start = ((), (), s32[]{:S(2)}) async-start(), calls=%async_computation.11 | async-start | bytes 4718592 | tf_op jit(solution)/shard_map/reduce_scatter | solution.py:82
  52.3 192.9 %reduce-scatter.11.cloned.1.call-start = ((), (), s32[]{:S(2)}) async-start(), calls=%async_computation.9 | async-start | bytes 327680 | tf_op jit(solution)/shard_map/reduce_scatter | solution.py:87
  82.1 164.6 %reduce-scatter.19.cloned.1.call-start = ((), (), s32[]{:S(2)}) async-start(), calls=%async_computation.13 | async-start | bytes 655360
  138.9 56.9 %copy-start.4 = (bf16[256,1024]{1,0:T(8,128)(2,1)S(1)}, bf16[256,1024]{1,0:T(8,128)(2,1)}, u32[]{:S(2)}) copy-start(bf16[256,1024]{1,0:T(8,128)(2,1)} %copy-done.3) | copy-start | bytes 1572868
  138.9 129.4 %reduce-scatter.17.cloned.1.call-start = ((), (), s32[]{:S(2)}) async-start(), calls=%async_computation.12 | async-start | bytes 655360 | tf_op jit(solution)/shard_map/reduce_scatter | solution.py:93
  192.0 153.7 %all-reduce.4.cloned.1.call-start = ((), (), s32[]{:S(2)}) async-start(), calls=%async_computation.14 | async-start | bytes 4194304 | tf_op jit(solution)/shard_map/psum | solution.py:69
  199.4 45.8 %all-to-all-start.1 = ((bf16[32,4,2048]{2,0,1:T(8,128)(2,1)}), bf16[32,4,2048]{2,0,1:T(8,128)(2,1)S(1)}, u32[]{:S(2)}, u32[]{:S(2)}) async-start(bf16[32,4,2048]{2,0,1:T(8,128)(2,1)} %copy.25), calls=%async_computation.1 | async-start | bytes 1048576 | tf_op jit(solution)/shard_map/all_to_all | solution.py:62
  345.6 3.1 copy-start.8
Sparse Core Ops, SparseCore 0:
  41.7 40.3 reduce-scatter.8
  85.5 51.3 reduce-scatter.12
  140.6 51.3 reduce-scatter.14
  194.0 24.2 reduce-scatter.10
  220.5 24.4 reduce-scatter.18
  247.2 21.0 reduce-scatter.16
Sparse Core Ops, SparseCore 1:
  198.5 147.1 all-reduce.3
where the time goes:
time: 358 us; the launch traced here: 357 us
  waiting for transfers between devices  246 us (69%)
  blocking collectives  41.2 us (12%)
  matrix products  22.1 us (6%)
  local copies, waits for them, and re-layouts  16.8 us (5%)
  between operations  15.8 us (4%)
  starting transfers between devices  11.5 us (3%)
    psum x1, waiting for transfers between devices, on_device(): lax.psum((emb_global_part, emb_local_part, gain_part), ('seq', 'tp'))  75.7 us
    reduce_scatter x1, waiting for transfers between devices, on_device(): lax.psum_scatter(up_part.astype(jnp.bfloat16), 'seq', scatter_dimension=1...  54.6 us
    reduce_scatter x1, waiting for transfers between devices, on_device(): lax.psum_scatter(down_part.astype(jnp.bfloat16), 'seq', scatter_dimension...  53 us
    psum x1, blocking collectives, on_device(): lax.psum((emb_global_part, emb_local_part, gain_part), ('seq', 'tp'))  41.2 us
    reduce_scatter x1, waiting for transfers between devices, on_device(): lax.psum_scatter(proj_part.astype(jnp.bfloat16), 'seq', scatter_dimension...  29.7 us
    reduce_scatter x1, waiting for transfers between devices, on_device(): lax.psum_scatter(down_half.astype(jnp.bfloat16), 'tp', scatter_dimension=...  19.7 us
    dot_general x5, matrix products, inner(): lax.dot_general(left, right, (((0,), (0,)), ((), ())), preferred_element_...  14.5 us
    all_to_all x1, waiting for transfers between devices, on_device(): lax.all_to_all(global_out, 'tp', split_axis=0, concat_axis=1, tiled=True)  13.5 us
  transfers between devices with their start and end apart: 9, of which 6 were waited for; matrix products, arithmetic and copies ran while one was open for 7% of the time, Pallas kernels for 0%

commit v1 on v0

v1 whole, which is shorter than its diff:
```python
import jax
import jax.numpy as jnp
from jax import lax
from jax.sharding import PartitionSpec as P

BF = jnp.bfloat16
F32 = jnp.float32


def inner(left, right):
    return lax.dot_general(
        left, right, (((0,), (0,)), ((), ())), preferred_element_type=F32
    )


def outer(left, right):
    return lax.dot_general(
        left, right, (((1,), (1,)), ((), ())), preferred_element_type=F32
    )


def times(left, right):
    return jnp.dot(left, right, preferred_element_type=F32)


def swap(value, axis, masks):
    count = lax.axis_size(axis)
    pairs = [(i, i ^ masks[i % len(masks)]) for i in range(count)]
    return lax.ppermute(value, axis, pairs)


def block_at(value, index, size, axis):
    return lax.dynamic_slice_in_dim(value, index * size, size, axis)


def tree(parts):
    while len(parts) > 1:
        parts = [parts[i] + parts[i + 1] for i in range(0, len(parts), 2)]
    return parts[0]


def on_device(
    byte_ids,
    global_out,
    global_in_grad,
    out_grad,
    proj_weight,
    emb_local,
    norm_gain,
    up_weight,
    down_weight,
):
    seq_count = lax.axis_size("seq")
    tp_count = lax.axis_size("tp")
    seq_place = lax.axis_index("seq")
    tp_place = lax.axis_index("tp")
    core = seq_place & 1
    chip = seq_place >> 1
    stages = seq_count.bit_length() - 2
    walks = (list(range(1, stages + 1)), list(range(stages, 0, -1)))
    patches, patch = byte_ids.shape
    slot, width = proj_weight.shape
    hidden = up_weight.shape[1]
    vocab = emb_local.shape[0]
    own = patch // tp_count
    part = patches // tp_count
    rows = own * patches

    def share_mask(number, walk):
        mask = 0
        for k in range(stages):
            if (number >> (stages - 1 - k)) & 1:
                mask |= 1 << (walk[k] - 1)
        return mask

    shares = [
        2 * (chip ^ jnp.where(core == 0, share_mask(n, walks[0]), share_mask(n, walks[1]))) + core
        for n in range(1 << stages)
    ]

    def stage_swap(value, k):
        return swap(value, "seq", (1 << walks[0][k], 1 << walks[1][k]))

    def core_swap(value):
        return swap(value, "seq", (1,))

    grad_by_slot = jnp.swapaxes(out_grad.reshape(part, patch, width), 0, 1).reshape(
        tp_count * own * part, width
    )
    out_own = jnp.zeros((own, tp_count, part, width), BF)
    for mask in range(tp_count):
        block = block_at(grad_by_slot, tp_place ^ mask, own * part, 0)
        if mask:
            block = swap(block, "tp", (mask,))
        out_own = lax.dynamic_update_slice(
            out_own, block.reshape(own, 1, part, width), (0, tp_place ^ mask, 0, 0)
        )
    out_own = out_own.reshape(rows, width)
    out_rows = jnp.concatenate([out_own, core_swap(out_own)], axis=0)

    def by_slot(value):
        other = core_swap(value)
        return jnp.concatenate(
            [part[:, j * slot : (j + 1) * slot] for part in (value, other) for j in range(own)],
            axis=0,
        )

    ids = byte_ids.T
    ids = jnp.concatenate([ids, core_swap(ids)], axis=1)
    before = jnp.concatenate([jnp.full((1, 2 * patches), -1, jnp.int32), ids[:-1]], axis=0)

    def of_rows(value):
        mine = lax.dynamic_slice_in_dim(value, tp_place * own, own, 0)
        return jnp.swapaxes(mine.reshape(own, 2, patches), 0, 1).reshape(2 * rows)

    own_ids = of_rows(ids)
    prev_ids = of_rows(before)
    prev_hot = (prev_ids[:, None] == jnp.arange(vocab)[None, :]).astype(BF)

    height = vocab // seq_count
    here = jnp.concatenate([share * height + jnp.arange(height) for share in shares])
    own_hot = (here[:, None] == own_ids[None, :]).astype(BF)
    prev_hot_here = (here[:, None] == prev_ids[None, :]).astype(BF)
    emb_global_part = times(own_hot, by_slot(global_in_grad))

    chunk = hidden // seq_count
    up_here = jnp.concatenate([block_at(up_weight, s, chunk, 1) for s in shares], axis=1)
    down_here = jnp.concatenate([block_at(down_weight, s, chunk, 0) for s in shares], axis=0)

    slot_in = by_slot(global_out)
    u_rows = times(slot_in, proj_weight) + times(prev_hot, emb_local)
    scale = lax.rsqrt(jnp.mean(u_rows * u_rows, axis=1, keepdims=True) + 1e-05)
    normed = u_rows * scale
    r_rows = (normed * norm_gain).astype(BF)
    a_rows = times(r_rows, up_here)
    sig = jax.nn.sigmoid(a_rows)
    h_rows = (a_rows * sig).astype(BF)

    def halving(keep, sent):
        for k in range(stages):
            value = keep + stage_swap(sent, k).astype(F32)
            size = value.shape[0] // 2
            if k + 1 < stages:
                keep, sent = value[:size], value[size:].astype(BF)
        return value

    def weight_sum(left, right):
        size = left.shape[1] // 2
        sent = inner(left[:, size:], right).astype(BF)
        keep = inner(left[:, :size], right)
        value = halving(keep, sent)
        size = value.shape[0] // tp_count
        parts = []
        for mask in range(tp_count):
            block = block_at(value, tp_place ^ mask, size, 0)
            if mask:
                block = swap(block.astype(BF), "tp", (mask,)).astype(F32)
            parts.append(block)
        return tree(parts)

    down_grad = weight_sum(h_rows, out_rows)
    dh_rows = outer(out_rows, down_here)
    da_rows = (dh_rows * sig * (1.0 + a_rows * (1.0 - sig))).astype(BF)
    up_grad = weight_sum(da_rows, r_rows).T
    dr_part = outer(da_rows, up_here)
    dr_sent = jnp.concatenate([dr_part[rows:], dr_part[:rows]], axis=0).astype(BF)
    dr_rows = dr_part + core_swap(dr_sent).astype(F32)
    gain_part = jnp.sum(dr_rows * normed, axis=0)
    dn_rows = dr_rows * norm_gain
    du_rows = (
        out_rows.astype(F32)
        + scale * (dn_rows - normed * jnp.mean(dn_rows * normed, axis=1, keepdims=True))
    ).astype(BF)

    emb_local_part = times(prev_hot_here, du_rows)
    strip = width // seq_count
    pieces = []
    for n, share in enumerate(shares):
        pieces.append(emb_global_part[n * height : (n + 1) * height])
        pieces.append(emb_local_part[n * height : (n + 1) * height])
        line = block_at(gain_part, share, strip, 0)[None]
        pieces.append(jnp.pad(line, ((0, 15), (0, width - strip))))
    tables = jnp.concatenate(pieces, axis=0)
    size = tables.shape[0] // 2
    value = halving(tables[:size], tables[size:].astype(BF)).astype(BF)
    parts = [swap(value, "tp", (mask,)) if mask else value for mask in range(tp_count)]
    value = tree([p.astype(F32) for p in parts]).astype(BF)
    for k in range(stages - 1, -1, -1):
        value = jnp.concatenate([value, stage_swap(value, k)], axis=0)
    both = jnp.stack([value, core_swap(value)]).reshape(2 << stages, -1, width)
    numbers = []
    for side in range(2):
        turn = core ^ side
        for n in range(1 << stages):
            mask = jnp.where(turn == 0, share_mask(n, walks[0]), share_mask(n, walks[1]))
            numbers.append(2 * (chip ^ mask) + turn)
    numbers = jnp.stack(numbers)
    where_from = (numbers[:, None] * height + jnp.arange(height)[None, :]).reshape(-1)
    sort = (jnp.arange(vocab)[:, None] == where_from[None, :]).astype(BF)
    emb_global_grad = times(sort, both[:, :height].reshape(vocab, width))
    emb_local_grad = times(sort, both[:, height : 2 * height].reshape(vocab, width))
    gain_sort = (jnp.arange(seq_count)[:, None] == numbers[None, :]).astype(BF)
    gain_grad = times(gain_sort, both[:, 2 * height, :strip]).reshape(width)

    columns = width // seq_count
    du_here = jnp.concatenate([block_at(du_rows, s, columns, 1) for s in shares], axis=1)
    proj_grad = weight_sum(du_here, slot_in).T
    back = outer(du_rows[:rows], proj_weight).astype(BF)
    glob_out_grad = jnp.concatenate(
        [back[j * patches : (j + 1) * patches] for j in range(own)], axis=1
    )
    return (
        glob_out_grad,
        emb_global_grad,
        emb_local_grad,
        gain_grad,
        proj_grad,
        up_grad,
        down_grad,
    )


def solution(mesh):
    placed = (
        P("seq", None),
        P("seq", "tp"),
        P("seq", "tp"),
        P(("seq", "tp"), None),
        P(),
        P(),
        P(),
        P(),
        P(),
    )
    return jax.shard_map(
        on_device,
        mesh=mesh,
        in_specs=placed,
        out_specs=(
            P("seq", "tp"),
            P(),
            P(),
            P(),
            P(None, ("seq", "tp")),
            P(None, ("seq", "tp")),
            P(("seq", "tp"), None),
        ),
        check_vma=False,
    )
```

time: 358 us -> 139 us (0.39)
  waiting for transfers between devices: 246 us -> 62.5 us
  blocking collectives: 41.2 us -> 0 us
  starting transfers between devices: 11.5 us -> 37.6 us
  between operations: 15.8 us -> 1.31 us
  matrix products: 22.1 us -> 16.3 us
    reduce_scatter x5 -> x0, waiting for transfers between devices: 157 us -> none  [the longest x1 54.6 us: on_device(): lax.psum_scatter(up_part.astype(jnp.bfloat16), 'seq', scatter_dimension=1...]
    psum x1 -> x0, waiting for transfers between devices: 75.7 us -> none  [on_device(): lax.psum((emb_global_part, emb_local_part, gain_part), ('seq', 'tp'))]
    ppermute x0 -> x31, waiting for transfers between devices: none -> 62.5 us  [swap(): return lax.ppermute(value, axis, pairs)]
    psum x1 -> x0, blocking collectives: 41.2 us -> none  [on_device(): lax.psum((emb_global_part, emb_local_part, gain_part), ('seq', 'tp'))]
    ppermute x0 -> x31, starting transfers between devices: none -> 37.6 us  [swap(): return lax.ppermute(value, axis, pairs)]
    all_to_all x2 -> x0, waiting for transfers between devices: 13.5 us -> none  [the longest x1 13.5 us: on_device(): lax.all_to_all(global_out, 'tp', split_axis=0, concat_axis=1, tiled=True)]
    all_to_all x2 -> x0, starting transfers between devices: 11.1 us -> none  [the longest x1 6.46 us: on_device(): lax.all_to_all(global_out, 'tp', split_axis=0, concat_axis=1, tiled=True)]
    dot_general x5 -> x6, matrix products: 14.5 us -> 3.87 us  [inner(): lax.dot_general(left, right, (((0,), (0,)), ((), ())), preferred_element_...]
  transfers between devices with their start and end apart: 9 -> 31, of which waited for: 6 -> 12; matrix products, arithmetic and copies ran while one was open for 7% -> 20% of each run, Pallas kernels for 0% -> 0%
where the time goes in v1:
time: 139 us
  waiting for transfers between devices  62.5 us (45%)
  starting transfers between devices  37.6 us (27%)
  matrix products  16.3 us (12%)
  local copies, waits for them, and re-layouts  15 us (11%)
  other arithmetic  5.84 us (4%)
    ppermute x31, waiting for transfers between devices, swap(): return lax.ppermute(value, axis, pairs)  62.5 us
    ppermute x31, starting transfers between devices, swap(): return lax.ppermute(value, axis, pairs)  37.6 us
    dot_general x8, matrix products, times(): return jnp.dot(left, right, preferred_element_type=F32)  8.36 us
    dynamic_slice x4, local copies, waits for them, and re-layouts, block_at(): return lax.dynamic_slice_in_dim(value, index * size, size, axis)  5.31 us
    dot_general x3, matrix products, outer(): lax.dot_general(left, right, (((1,), (1,)), ((), ())), preferred_element_...  4.11 us
    dot_general x6, matrix products, inner(): lax.dot_general(left, right, (((0,), (0,)), ((), ())), preferred_element_...  3.87 us
    slice x4, local copies, waits for them, and re-layouts, by_slot(): part[:, j * slot:(j + 1) * slot]  3.68 us
  transfers between devices with their start and end apart: 31, of which 12 were waited for; matrix products, arithmetic and copies ran while one was open for 20% of the time, Pallas kernels for 0%

profile of v1, /device:TPU:0, one launch (start us, length us, event | category | flops | bytes accessed | tf_op | source)
XLA Modules:
  0.0 138.7 jit_solution(3556150201290429099)
XLA Ops:
  3.4 3.0 %collective-permute-start = (bf16[64,1024]{1,0:T(8,128)(2,1)}, bf16[64,1024]{1,0:T(8,128)(2,1)}, u32[]{:S(2)}, u32[]{:S(2)}) collective-permute-start(bf16[64,1024]{1,0:T(8,128)(2,1)} %get-tuple-element.44), channel_id=1, source_target_pairs={{0,1},{1,0},{2,3},{3,2},{4,5},{5,4},{6,7},{7,6},{8,9},{9,8},{10,11... | collective-permute-start | bytes 393224 | tf_op jit(solution)/shard_map/ppermute | solution.py:29
  6.4 2.6 %collective-permute-start.1 = (bf16[64,1024]{1,0:T(8,128)(2,1)}, bf16[64,1024]{1,0:T(8,128)(2,1)}, u32[]{:S(2)}, u32[]{:S(2)}) collective-permute-start(bf16[64,1024]{1,0:T(8,128)(2,1)} %get-tuple-element.43), channel_id=1, source_target_pairs={{0,2},{1,3},{2,0},{3,1},{4,6},{5,7},{6,4},{7,5},{8,10},{9,11},{10,... | collective-permute-start | bytes 393224 | tf_op jit(solution)/shard_map/ppermute | solution.py:29
  9.7 1.8 %fusion.60 = (bf16[128,1024]{1,0:T(8,128)(2,1)}, bf16[128,1024]{1,0:T(8,128)(2,1)}) fusion(bf16[128,2048]{1,0:T(8,128)(2,1)} %param.11), kind=kLoop, calls=%fused_computation.158 | loop fusion | bytes 1048576 | tf_op jit(solution)/shard_map/slice | solution.py:104
  11.5 3.1 %constant_dynamic-slice_fusion.7 = (bf16[1024,256]{1,0:T(8,128)(2,1)}, bf16[1024,256]{1,0:T(8,128)(2,1)}, bf16[1024,256]{1,0:T(8,128)(2,1)}, bf16[1024,256]{1,0:T(8,128)(2,1)}) fusion(bf16[1024,2048]{1,0:T(8,128)(2,1)} %param.16, s32[]{:T(128)S(6)} %select_n.110, s32[]{:T(128)S(6)} %select_n.112, s32[]{:T(128)S(6)} %select_n.115, s32[]{:T(128)S(6)} %select_n.114), kind=kLoop, calls=%fused_computation.117 | loop fusion | bytes 4194320 | tf_op jit(solution)/shard_map/dynamic_slice | solution.py:33
  14.8 1.4 constant_dynamic-slice_fusion.11
  16.8 1.6 %fusion.26 = f32[512,1024]{1,0:T(8,128)S(1)} fusion(bf16[256,1024]{1,0:T(8,128)(2,1)} %param.14, s32[512]{0:T(512)S(1)} %bitcast.81), kind=kOutput, calls=%fused_computation.55 | convolution fusion | flops 268566528 | bytes 2623488 | tf_op jit(solution)/shard_map/dot_general | solution.py:23
  20.2 4.5 %collective-permute-done.2 = bf16[64,1024]{1,0:T(8,128)(2,1)S(1)} collective-permute-done((bf16[64,1024]{1,0:T(8,128)(2,1)}, bf16[64,1024]{1,0:T(8,128)(2,1)S(1)}, u32[]{:S(2)}, u32[]{:S(2)}) %collective-permute-start.2) | collective-permute-done | bytes 131104 | tf_op jit(solution)/shard_map/ppermute | solution.py:29
  25.9 1.3 multiply_reduce_fusion.2
  28.8 1.5 %multiply_convert_fusion = (bf16[512,1024]{1,0:T(8,128)(2,1)S(1)}, f32[512,1024]{1,0:T(8,128)S(1)}) fusion(bf16[512,1024]{1,0:T(8,128)(2,1)S(1)} %multiply_convert_fusion.2, bf16[1024,256]{1,0:T(8,128)(2,1)S(1)} %copy-done.5, bf16[1024,256]{1,0:T(8,128)(2,1)S(1)} %copy-done.6, bf16[1024,256]{1,0:T(8,128)(2,1)S(1)} %copy-done.4, ...), kind=kOutput, calls=%fused_computation.10 | convolution fusion | flops 1084751872 | bytes 6291456 | tf_op jit(solution)/shard_map/dot_general | solution.py:23
  30.4 1.6 %multiply_convert_fusion.1 = bf16[512,1024]{1,0:T(8,128)(2,1)S(1)} fusion(f32[512,1024]{1,0:T(8,128)S(1)} %get-tuple-element.63, bf16[256,1024]{1,0:T(8,128)(2,1)S(1)} %copy-done.9, bf16[256,1024]{1,0:T(8,128)(2,1)S(1)} %copy-done.10, bf16[256,1024]{1,0:T(8,128)(2,1)S(1)} %copy-done.8, bf16[256,1024]{1,0:T(8,128)(2,1)S(1)} %copy-done.7, ...), kind=kOutput, calls=%fused_computation.16 | convolution fusion | flops 1088946176 | bytes 6291456 | tf_op jit(solution)/shard_map/dot_general | solution.py:17
  32.0 1.7 %fusion.65 = (bf16[512,1024]{1,0:T(8,128)(2,1)S(1)}, f32[512,1024]{1,0:T(8,128)S(1)}) fusion(bf16[512,1024]{1,0:T(8,128)(2,1)S(1)} %multiply_convert_fusion.1, bf16[1024,256]{1,0:T(8,128)(2,1)S(1)} %copy-done.5, bf16[1024,256]{1,0:T(8,128)(2,1)S(1)} %copy-done.6, bf16[1024,256]{1,0:T(8,128)(2,1)S(1)} %copy-done.4, bf16[1024,256]{1,0:T(8,128)(2,1)S(1)} %copy-done.3), kind=kOutput, calls=%fused_computation.163 | convolution fusion | flops 1082654720 | bytes 6291456 | tf_op jit(solution)/shard_map/dot_general | solution.py:17
  35.9 1.6 %collective-permute-start.21 = (bf16[512,1024]{1,0:T(8,128)(2,1)S(1)}, bf16[512,1024]{1,0:T(8,128)(2,1)S(1)}, u32[]{:S(2)}, u32[]{:S(2)}) collective-permute-start(bf16[512,1024]{1,0:T(8,128)(2,1)S(1)} %convolution_convert_fusion.1), channel_id=1, source_target_pairs={{0,8},{4,20},{8,0},{12,28},{16,24},{20,4},{24,16},{28,12},{1,9},{5... | collective-permute-start | bytes 3145736 | tf_op jit(solution)/shard_map/ppermute | solution.py:29
  40.7 1.6 %collective-permute-start.8 = (bf16[160,1024]{1,0:T(8,128)(2,1)S(1)}, bf16[160,1024]{1,0:T(8,128)(2,1)S(1)}, u32[]{:S(2)}, u32[]{:S(2)}) collective-permute-start(bf16[160,1024]{1,0:T(8,128)(2,1)S(1)} %pad_dynamic-update-slice_fusion.2), channel_id=1, source_target_pairs={{0,8},{4,20},{8,0},{12,28},{16,24},{20,4},{24,16},{28,12},{1,9},{5... | collective-permute-start | bytes 983048 | tf_op jit(solution)/shard_map/ppermute | solution.py:29
  43.4 7.3 %collective-permute-done.21 = bf16[512,1024]{1,0:T(8,128)(2,1)S(1)} collective-permute-done((bf16[512,1024]{1,0:T(8,128)(2,1)S(1)}, bf16[512,1024]{1,0:T(8,128)(2,1)S(1)}, u32[]{:S(2)}, u32[]{:S(2)}) %collective-permute-start.21) | collective-permute-done | bytes 1048608 | tf_op jit(solution)/shard_map/ppermute | solution.py:29
  51.6 1.6 %collective-permute-start.22 = (bf16[256,1024]{1,0:T(8,128)(2,1)S(1)}, bf16[256,1024]{1,0:T(8,128)(2,1)S(1)}, u32[]{:S(2)}, u32[]{:S(2)}) collective-permute-start(bf16[256,1024]{1,0:T(8,128)(2,1)S(1)} %slice.237), channel_id=1, source_target_pairs={{0,16},{4,12},{8,24},{12,4},{16,0},{20,28},{24,8},{28,20},{1,17},{... | collective-permute-start | bytes 1572872 | tf_op jit(solution)/shard_map/ppermute | solution.py:29
  54.1 13.6 %collective-permute-done.26 = bf16[512,1024]{1,0:T(8,128)(2,1)S(1)} collective-permute-done((bf16[512,1024]{1,0:T(8,128)(2,1)S(1)}, bf16[512,1024]{1,0:T(8,128)(2,1)S(1)}, u32[]{:S(2)}, u32[]{:S(2)}) %collective-permute-start.26) | collective-permute-done | bytes 1048608 | tf_op jit(solution)/shard_map/ppermute | solution.py:29
  68.5 1.6 %collective-permute-start.27 = (bf16[256,1024]{1,0:T(8,128)(2,1)S(1)}, bf16[256,1024]{1,0:T(8,128)(2,1)S(1)}, u32[]{:S(2)}, u32[]{:S(2)}) collective-permute-start(bf16[256,1024]{1,0:T(8,128)(2,1)S(1)} %slice.236), channel_id=1, source_target_pairs={{0,16},{4,12},{8,24},{12,4},{16,0},{20,28},{24,8},{28,20},{1,17},{... | collective-permute-start | bytes 1572872 | tf_op jit(solution)/shard_map/ppermute | solution.py:29
  71.5 1.6 %collective-permute-start.9 = (bf16[80,1024]{1,0:T(8,128)(2,1)S(1)}, bf16[80,1024]{1,0:T(8,128)(2,1)S(1)}, u32[]{:S(2)}, u32[]{:S(2)}) collective-permute-start(bf16[80,1024]{1,0:T(8,128)(2,1)S(1)} %slice.239), channel_id=1, source_target_pairs={{0,16},{4,12},{8,24},{12,4},{16,0},{20,28},{24,8},{28,20},{1,17},{... | collective-permute-start | bytes 491528 | tf_op jit(solution)/shard_map/ppermute | solution.py:29
  74.0 9.7 %collective-permute-done.9 = bf16[80,1024]{1,0:T(8,128)(2,1)S(1)} collective-permute-done((bf16[80,1024]{1,0:T(8,128)(2,1)S(1)}, bf16[80,1024]{1,0:T(8,128)(2,1)S(1)}, u32[]{:S(2)}, u32[]{:S(2)}) %collective-permute-start.9) | collective-permute-done | bytes 163872 | tf_op jit(solution)/shard_map/ppermute | solution.py:29
  84.0 2.5 %collective-permute-start.11 = (bf16[80,1024]{1,0:T(8,128)(2,1)S(1)}, bf16[80,1024]{1,0:T(8,128)(2,1)S(1)}, u32[]{:S(2)}, u32[]{:S(2)}) collective-permute-start(bf16[80,1024]{1,0:T(8,128)(2,1)S(1)} %fusion.29), channel_id=1, source_target_pairs={{0,2},{1,3},{2,0},{3,1},{4,6},{5,7},{6,4},{7,5},{8,10},{9,11},{10,... | collective-permute-start | bytes 491528 | tf_op jit(solution)/shard_map/ppermute | solution.py:29
  86.5 1.6 %collective-permute-start.10 = (bf16[80,1024]{1,0:T(8,128)(2,1)S(1)}, bf16[80,1024]{1,0:T(8,128)(2,1)S(1)}, u32[]{:S(2)}, u32[]{:S(2)}) collective-permute-start(bf16[80,1024]{1,0:T(8,128)(2,1)S(1)} %fusion.29), channel_id=1, source_target_pairs={{0,1},{1,0},{2,3},{3,2},{4,5},{5,4},{6,7},{7,6},{8,9},{9,8},{10,11... | collective-permute-start | bytes 491528 | tf_op jit(solution)/shard_map/ppermute | solution.py:29
  88.6 1.6 %collective-permute-start.17 = (bf16[128,1024]{1,0:T(8,128)(2,1)S(1)}, bf16[128,1024]{1,0:T(8,128)(2,1)S(1)}, u32[]{:S(2)}, u32[]{:S(2)}) collective-permute-start(bf16[128,1024]{1,0:T(8,128)(2,1)S(1)} %slice.238), channel_id=1, source_target_pairs={{0,16},{4,12},{8,24},{12,4},{16,0},{20,28},{24,8},{28,20},{1,17},{... | collective-permute-start | bytes 786440 | tf_op jit(solution)/shard_map/ppermute | solution.py:29
  90.4 2.3 %collective-permute-done.12 = bf16[80,1024]{1,0:T(8,128)(2,1)S(1)} collective-permute-done((bf16[80,1024]{1,0:T(8,128)(2,1)S(1)}, bf16[80,1024]{1,0:T(8,128)(2,1)S(1)}, u32[]{:S(2)}, u32[]{:S(2)}) %collective-permute-start.12) | collective-permute-done | bytes 163872 | tf_op jit(solution)/shard_map/ppermute | solution.py:29
  92.9 11.9 %collective-permute-done.11 = bf16[80,1024]{1,0:T(8,128)(2,1)S(1)} collective-permute-done((bf16[80,1024]{1,0:T(8,128)(2,1)S(1)}, bf16[80,1024]{1,0:T(8,128)(2,1)S(1)}, u32[]{:S(2)}, u32[]{:S(2)}) %collective-permute-start.11) | collective-permute-done | bytes 163872 | tf_op jit(solution)/shard_map/ppermute | solution.py:29
  106.3 1.6 %collective-permute-start.13 = (bf16[80,1024]{1,0:T(8,128)(2,1)S(1)}, bf16[80,1024]{1,0:T(8,128)(2,1)S(1)}, u32[]{:S(2)}, u32[]{:S(2)}) collective-permute-start(bf16[80,1024]{1,0:T(8,128)(2,1)S(1)} %add_convert_fusion.1), channel_id=1, source_target_pairs={{0,16},{4,12},{8,24},{12,4},{16,0},{20,28},{24,8},{28,20},{1,17},{... | collective-permute-start | bytes 491528 | tf_op jit(solution)/shard_map/ppermute | solution.py:29
  108.1 3.6 %collective-permute-done.13 = bf16[80,1024]{1,0:T(8,128)(2,1)S(1)} collective-permute-done((bf16[80,1024]{1,0:T(8,128)(2,1)S(1)}, bf16[80,1024]{1,0:T(8,128)(2,1)S(1)}, u32[]{:S(2)}, u32[]{:S(2)}) %collective-permute-start.13) | collective-permute-done | bytes 163872 | tf_op jit(solution)/shard_map/ppermute | solution.py:29
  111.7 1.6 %collective-permute-start.14 = (bf16[160,1024]{1,0:T(8,128)(2,1)S(1)}, bf16[160,1024]{1,0:T(8,128)(2,1)S(1)}, u32[]{:S(2)}, u32[]{:S(2)}) collective-permute-start(bf16[160,1024]{1,0:T(8,128)(2,1)S(1)} %pad_maximum_fusion.9), channel_id=1, source_target_pairs={{0,8},{4,20},{8,0},{12,28},{16,24},{20,4},{24,16},{28,12},{1,9},{5... | collective-permute-start | bytes 983048 | tf_op jit(solution)/shard_map/ppermute | solution.py:29
  113.3 3.1 %collective-permute-start.30 = (bf16[64,1024]{1,0:T(8,128)(2,1)S(1)}, bf16[64,1024]{1,0:T(8,128)(2,1)S(1)}, u32[]{:S(2)}, u32[]{:S(2)}) collective-permute-start(bf16[64,1024]{1,0:T(8,128)(2,1)S(1)} %get-tuple-element.20), channel_id=1, source_target_pairs={{0,3},{1,2},{2,1},{3,0},{4,7},{5,6},{6,5},{7,4},{8,11},{9,10},{10,... | collective-permute-start | bytes 393224 | tf_op jit(solution)/shard_map/ppermute | solution.py:29
  119.2 3.1 %collective-permute-start.20 = (bf16[32,1024]{1,0:T(8,128)(2,1)S(1)}, bf16[32,1024]{1,0:T(8,128)(2,1)S(1)}, u32[]{:S(2)}, u32[]{:S(2)}) collective-permute-start(bf16[32,1024]{1,0:T(8,128)(2,1)S(1)} %get-tuple-element.34), channel_id=1, source_target_pairs={{0,3},{1,2},{2,1},{3,0},{4,7},{5,6},{6,5},{7,4},{8,11},{9,10},{10,... | collective-permute-start | bytes 196616 | tf_op jit(solution)/shard_map/ppermute | solution.py:29
  122.4 3.3 %collective-permute-start.19 = (bf16[32,1024]{1,0:T(8,128)(2,1)S(1)}, bf16[32,1024]{1,0:T(8,128)(2,1)S(1)}, u32[]{:S(2)}, u32[]{:S(2)}) collective-permute-start(bf16[32,1024]{1,0:T(8,128)(2,1)S(1)} %get-tuple-element.35), channel_id=1, source_target_pairs={{0,2},{1,3},{2,0},{3,1},{4,6},{5,7},{6,4},{7,5},{8,10},{9,11},{10,... | collective-permute-start | bytes 196616 | tf_op jit(solution)/shard_map/ppermute | solution.py:29
  125.7 4.5 %collective-permute-done.29 = bf16[64,1024]{1,0:T(8,128)(2,1)S(1)} collective-permute-done((bf16[64,1024]{1,0:T(8,128)(2,1)S(1)}, bf16[64,1024]{1,0:T(8,128)(2,1)S(1)}, u32[]{:S(2)}, u32[]{:S(2)}) %collective-permute-start.29) | collective-permute-done | bytes 131104 | tf_op jit(solution)/shard_map/ppermute | solution.py:29
  131.6 2.9 %collective-permute-done.18 = bf16[32,1024]{1,0:T(8,128)(2,1)S(1)} collective-permute-done((bf16[32,1024]{1,0:T(8,128)(2,1)S(1)}, bf16[32,1024]{1,0:T(8,128)(2,1)S(1)}, u32[]{:S(2)}, u32[]{:S(2)}) %collective-permute-start.18) | collective-permute-done | bytes 65568 | tf_op jit(solution)/shard_map/ppermute | solution.py:29
  (147 shorter events, 31.2 us)
Async XLA Ops:
  0.6 25.2 %copy-start = (bf16[1024,1024]{1,0:T(8,128)(2,1)S(1)}, bf16[1024,1024]{1,0:T(8,128)(2,1)}, u32[]{:S(2)}) copy-start(bf16[1024,1024]{1,0:T(8,128)(2,1)} %param.13) | copy-start | bytes 6291460
  0.7 16.0 %collective-permute-start.5 = (s32[8,128]{1,0:T(8,128)}, s32[8,128]{1,0:T(8,128)S(1)}, u32[]{:S(2)}, u32[]{:S(2)}) collective-permute-start(s32[8,128]{1,0:T(8,128)} %bitcast.83), channel_id=1, source_target_pairs={{0,4},{4,0},{8,12},{12,8},{16,20},{20,16},{24,28},{28,24},{1,5},{5... | collective-permute-start | bytes 12296 | tf_op jit(solution)/shard_map/ppermute | solution.py:29
  1.2 23.6 %collective-permute-start.4 = (bf16[128,2048]{1,0:T(8,128)(2,1)}, bf16[128,2048]{1,0:T(8,128)(2,1)}, u32[]{:S(2)}, u32[]{:S(2)}) collective-permute-start(bf16[128,2048]{1,0:T(8,128)(2,1)} %param.10), channel_id=1, source_target_pairs={{0,4},{4,0},{8,12},{12,8},{16,20},{20,16},{24,28},{28,24},{1,5},{5... | collective-permute-start | bytes 1572872 | tf_op jit(solution)/shard_map/ppermute | solution.py:29
  3.4 15.0 %collective-permute-start = (bf16[64,1024]{1,0:T(8,128)(2,1)}, bf16[64,1024]{1,0:T(8,128)(2,1)}, u32[]{:S(2)}, u32[]{:S(2)}) collective-permute-start(bf16[64,1024]{1,0:T(8,128)(2,1)} %get-tuple-element.44), channel_id=1, source_target_pairs={{0,1},{1,0},{2,3},{3,2},{4,5},{5,4},{6,7},{7,6},{8,9},{9,8},{10,11... | collective-permute-start | bytes 393224 | tf_op jit(solution)/shard_map/ppermute | solution.py:29
  6.4 12.9 %collective-permute-start.1 = (bf16[64,1024]{1,0:T(8,128)(2,1)}, bf16[64,1024]{1,0:T(8,128)(2,1)}, u32[]{:S(2)}, u32[]{:S(2)}) collective-permute-start(bf16[64,1024]{1,0:T(8,128)(2,1)} %get-tuple-element.43), channel_id=1, source_target_pairs={{0,2},{1,3},{2,0},{3,1},{4,6},{5,7},{6,4},{7,5},{8,10},{9,11},{10,... | collective-permute-start | bytes 393224 | tf_op jit(solution)/shard_map/ppermute | solution.py:29
  9.0 18.6 %collective-permute-start.7 = (bf16[128,2048]{1,0:T(8,128)(2,1)}, bf16[128,2048]{1,0:T(8,128)(2,1)S(1)}, u32[]{:S(2)}, u32[]{:S(2)}) collective-permute-start(bf16[128,2048]{1,0:T(8,128)(2,1)} %param.11), channel_id=1, source_target_pairs={{0,4},{4,0},{8,12},{12,8},{16,20},{20,16},{24,28},{28,24},{1,5},{5... | collective-permute-start | bytes 1572872 | tf_op jit(solution)/shard_map/ppermute | solution.py:29
  16.6 8.1 %collective-permute-start.2 = (bf16[64,1024]{1,0:T(8,128)(2,1)}, bf16[64,1024]{1,0:T(8,128)(2,1)S(1)}, u32[]{:S(2)}, u32[]{:S(2)}) collective-permute-start(bf16[64,1024]{1,0:T(8,128)(2,1)} %get-tuple-element.42), channel_id=1, source_target_pairs={{0,3},{1,2},{2,1},{3,0},{4,7},{5,6},{6,5},{7,4},{8,11},{9,10},{10,... | collective-permute-start | bytes 393224 | tf_op jit(solution)/shard_map/ppermute | solution.py:29
  24.7 5.6 %collective-permute-start.3 = (bf16[256,1024]{1,0:T(8,128)(2,1)S(1)}, bf16[256,1024]{1,0:T(8,128)(2,1)S(1)}, u32[]{:S(2)}, u32[]{:S(2)}) collective-permute-start(bf16[256,1024]{1,0:T(8,128)(2,1)S(1)} %bitcast.69), channel_id=1, source_target_pairs={{0,4},{4,0},{8,12},{12,8},{16,20},{20,16},{24,28},{28,24},{1,5},{5... | collective-permute-start | bytes 1572872 | tf_op jit(solution)/shard_map/ppermute | solution.py:29
  33.9 4.9 %collective-permute-start.6 = (bf16[512,1024]{1,0:T(8,128)(2,1)S(1)}, bf16[512,1024]{1,0:T(8,128)(2,1)S(1)}, u32[]{:S(2)}, u32[]{:S(2)}) collective-permute-start(bf16[512,1024]{1,0:T(8,128)(2,1)S(1)} %pad_maximum_fusion.4), channel_id=1, source_target_pairs={{0,4},{4,0},{8,12},{12,8},{16,20},{20,16},{24,28},{28,24},{1,5},{5... | collective-permute-start | bytes 3145736 | tf_op jit(solution)/shard_map/ppermute | solution.py:29
  35.9 14.9 %collective-permute-start.21 = (bf16[512,1024]{1,0:T(8,128)(2,1)S(1)}, bf16[512,1024]{1,0:T(8,128)(2,1)S(1)}, u32[]{:S(2)}, u32[]{:S(2)}) collective-permute-start(bf16[512,1024]{1,0:T(8,128)(2,1)S(1)} %convolution_convert_fusion.1), channel_id=1, source_target_pairs={{0,8},{4,20},{8,0},{12,28},{16,24},{20,4},{24,16},{28,12},{1,9},{5... | collective-permute-start | bytes 3145736 | tf_op jit(solution)/shard_map/ppermute | solution.py:29
  38.2 29.4 %collective-permute-start.26 = (bf16[512,1024]{1,0:T(8,128)(2,1)S(1)}, bf16[512,1024]{1,0:T(8,128)(2,1)S(1)}, u32[]{:S(2)}, u32[]{:S(2)}) collective-permute-start(bf16[512,1024]{1,0:T(8,128)(2,1)S(1)} %convolution_convert_fusion), channel_id=1, source_target_pairs={{0,8},{4,20},{8,0},{12,28},{16,24},{20,4},{24,16},{28,12},{1,9},{5... | collective-permute-start | bytes 3145736 | tf_op jit(solution)/shard_map/ppermute | solution.py:29
  40.7 30.7 %collective-permute-start.8 = (bf16[160,1024]{1,0:T(8,128)(2,1)S(1)}, bf16[160,1024]{1,0:T(8,128)(2,1)S(1)}, u32[]{:S(2)}, u32[]{:S(2)}) collective-permute-start(bf16[160,1024]{1,0:T(8,128)(2,1)S(1)} %pad_dynamic-update-slice_fusion.2), channel_id=1, source_target_pairs={{0,8},{4,20},{8,0},{12,28},{16,24},{20,4},{24,16},{28,12},{1,9},{5... | collective-permute-start | bytes 983048 | tf_op jit(solution)/shard_map/ppermute | solution.py:29
  42.8 43.7 %collective-permute-start.16 = (bf16[256,1024]{1,0:T(8,128)(2,1)S(1)}, bf16[256,1024]{1,0:T(8,128)(2,1)S(1)}, u32[]{:S(2)}, u32[]{:S(2)}) collective-permute-start(bf16[256,1024]{1,0:T(8,128)(2,1)S(1)} %convolution_convert_fusion.2), channel_id=1, source_target_pairs={{0,8},{4,20},{8,0},{12,28},{16,24},{20,4},{24,16},{28,12},{1,9},{5... | collective-permute-start | bytes 1572872 | tf_op jit(solution)/shard_map/ppermute | solution.py:29
  51.6 37.0 %collective-permute-start.22 = (bf16[256,1024]{1,0:T(8,128)(2,1)S(1)}, bf16[256,1024]{1,0:T(8,128)(2,1)S(1)}, u32[]{:S(2)}, u32[]{:S(2)}) collective-permute-start(bf16[256,1024]{1,0:T(8,128)(2,1)S(1)} %slice.237), channel_id=1, source_target_pairs={{0,16},{4,12},{8,24},{12,4},{16,0},{20,28},{24,8},{28,20},{1,17},{... | collective-permute-start | bytes 1572872 | tf_op jit(solution)/shard_map/ppermute | solution.py:29
  68.5 37.8 %collective-permute-start.27 = (bf16[256,1024]{1,0:T(8,128)(2,1)S(1)}, bf16[256,1024]{1,0:T(8,128)(2,1)S(1)}, u32[]{:S(2)}, u32[]{:S(2)}) collective-permute-start(bf16[256,1024]{1,0:T(8,128)(2,1)S(1)} %slice.236), channel_id=1, source_target_pairs={{0,16},{4,12},{8,24},{12,4},{16,0},{20,28},{24,8},{28,20},{1,17},{... | collective-permute-start | bytes 1572872 | tf_op jit(solution)/shard_map/ppermute | solution.py:29
  71.5 12.1 %collective-permute-start.9 = (bf16[80,1024]{1,0:T(8,128)(2,1)S(1)}, bf16[80,1024]{1,0:T(8,128)(2,1)S(1)}, u32[]{:S(2)}, u32[]{:S(2)}) collective-permute-start(bf16[80,1024]{1,0:T(8,128)(2,1)S(1)} %slice.239), channel_id=1, source_target_pairs={{0,16},{4,12},{8,24},{12,4},{16,0},{20,28},{24,8},{28,20},{1,17},{... | collective-permute-start | bytes 491528 | tf_op jit(solution)/shard_map/ppermute | solution.py:29
  83.7 9.0 %collective-permute-start.12 = (bf16[80,1024]{1,0:T(8,128)(2,1)S(1)}, bf16[80,1024]{1,0:T(8,128)(2,1)S(1)}, u32[]{:S(2)}, u32[]{:S(2)}) collective-permute-start(bf16[80,1024]{1,0:T(8,128)(2,1)S(1)} %fusion.29), channel_id=1, source_target_pairs={{0,3},{1,2},{2,1},{3,0},{4,7},{5,6},{6,5},{7,4},{8,11},{9,10},{10,... | collective-permute-start | bytes 491528 | tf_op jit(solution)/shard_map/ppermute | solution.py:29
  84.0 20.9 %collective-permute-start.11 = (bf16[80,1024]{1,0:T(8,128)(2,1)S(1)}, bf16[80,1024]{1,0:T(8,128)(2,1)S(1)}, u32[]{:S(2)}, u32[]{:S(2)}) collective-permute-start(bf16[80,1024]{1,0:T(8,128)(2,1)S(1)} %fusion.29), channel_id=1, source_target_pairs={{0,2},{1,3},{2,0},{3,1},{4,6},{5,7},{6,4},{7,5},{8,10},{9,11},{10,... | collective-permute-start | bytes 491528 | tf_op jit(solution)/shard_map/ppermute | solution.py:29
  86.5 18.3 %collective-permute-start.10 = (bf16[80,1024]{1,0:T(8,128)(2,1)S(1)}, bf16[80,1024]{1,0:T(8,128)(2,1)S(1)}, u32[]{:S(2)}, u32[]{:S(2)}) collective-permute-start(bf16[80,1024]{1,0:T(8,128)(2,1)S(1)} %fusion.29), channel_id=1, source_target_pairs={{0,1},{1,0},{2,3},{3,2},{4,5},{5,4},{6,7},{7,6},{8,9},{9,8},{10,11... | collective-permute-start | bytes 491528 | tf_op jit(solution)/shard_map/ppermute | solution.py:29
  88.6 30.5 %collective-permute-start.17 = (bf16[128,1024]{1,0:T(8,128)(2,1)S(1)}, bf16[128,1024]{1,0:T(8,128)(2,1)S(1)}, u32[]{:S(2)}, u32[]{:S(2)}) collective-permute-start(bf16[128,1024]{1,0:T(8,128)(2,1)S(1)} %slice.238), channel_id=1, source_target_pairs={{0,16},{4,12},{8,24},{12,4},{16,0},{20,28},{24,8},{28,20},{1,17},{... | collective-permute-start | bytes 786440 | tf_op jit(solution)/shard_map/ppermute | solution.py:29
  92.7 20.6 %collective-permute-start.25 = (bf16[64,1024]{1,0:T(8,128)(2,1)S(1)}, bf16[64,1024]{1,0:T(8,128)(2,1)S(1)}, u32[]{:S(2)}, u32[]{:S(2)}) collective-permute-start(bf16[64,1024]{1,0:T(8,128)(2,1)S(1)} %get-tuple-element.23), channel_id=1, source_target_pairs={{0,3},{1,2},{2,1},{3,0},{4,7},{5,6},{6,5},{7,4},{8,11},{9,10},{10,... | collective-permute-start | bytes 393224 | tf_op jit(solution)/shard_map/ppermute | solution.py:29
  104.9 11.6 %collective-permute-start.24 = (bf16[64,1024]{1,0:T(8,128)(2,1)S(1)}, bf16[64,1024]{1,0:T(8,128)(2,1)S(1)}, u32[]{:S(2)}, u32[]{:S(2)}) collective-permute-start(bf16[64,1024]{1,0:T(8,128)(2,1)S(1)} %get-tuple-element.24), channel_id=1, source_target_pairs={{0,2},{1,3},{2,0},{3,1},{4,6},{5,7},{6,4},{7,5},{8,10},{9,11},{10,... | collective-permute-start | bytes 393224 | tf_op jit(solution)/shard_map/ppermute | solution.py:29
  104.9 11.6 %collective-permute-start.23 = (bf16[64,1024]{1,0:T(8,128)(2,1)S(1)}, bf16[64,1024]{1,0:T(8,128)(2,1)S(1)}, u32[]{:S(2)}, u32[]{:S(2)}) collective-permute-start(bf16[64,1024]{1,0:T(8,128)(2,1)S(1)} %get-tuple-element.22), channel_id=1, source_target_pairs={{0,1},{1,0},{2,3},{3,2},{4,5},{5,4},{6,7},{7,6},{8,9},{9,8},{10,11... | collective-permute-start | bytes 393224 | tf_op jit(solution)/shard_map/ppermute | solution.py:29
  106.3 5.4 %collective-permute-start.13 = (bf16[80,1024]{1,0:T(8,128)(2,1)S(1)}, bf16[80,1024]{1,0:T(8,128)(2,1)S(1)}, u32[]{:S(2)}, u32[]{:S(2)}) collective-permute-start(bf16[80,1024]{1,0:T(8,128)(2,1)S(1)} %add_convert_fusion.1), channel_id=1, source_target_pairs={{0,16},{4,12},{8,24},{12,4},{16,0},{20,28},{24,8},{28,20},{1,17},{... | collective-permute-start | bytes 491528 | tf_op jit(solution)/shard_map/ppermute | solution.py:29
  111.7 7.1 %collective-permute-start.14 = (bf16[160,1024]{1,0:T(8,128)(2,1)S(1)}, bf16[160,1024]{1,0:T(8,128)(2,1)S(1)}, u32[]{:S(2)}, u32[]{:S(2)}) collective-permute-start(bf16[160,1024]{1,0:T(8,128)(2,1)S(1)} %pad_maximum_fusion.9), channel_id=1, source_target_pairs={{0,8},{4,20},{8,0},{12,28},{16,24},{20,4},{24,16},{28,12},{1,9},{5... | collective-permute-start | bytes 983048 | tf_op jit(solution)/shard_map/ppermute | solution.py:29
  113.3 9.0 %collective-permute-start.30 = (bf16[64,1024]{1,0:T(8,128)(2,1)S(1)}, bf16[64,1024]{1,0:T(8,128)(2,1)S(1)}, u32[]{:S(2)}, u32[]{:S(2)}) collective-permute-start(bf16[64,1024]{1,0:T(8,128)(2,1)S(1)} %get-tuple-element.20), channel_id=1, source_target_pairs={{0,3},{1,2},{2,1},{3,0},{4,7},{5,6},{6,5},{7,4},{8,11},{9,10},{10,... | collective-permute-start | bytes 393224 | tf_op jit(solution)/shard_map/ppermute | solution.py:29
  116.5 13.7 %collective-permute-start.29 = (bf16[64,1024]{1,0:T(8,128)(2,1)S(1)}, bf16[64,1024]{1,0:T(8,128)(2,1)S(1)}, u32[]{:S(2)}, u32[]{:S(2)}) collective-permute-start(bf16[64,1024]{1,0:T(8,128)(2,1)S(1)} %get-tuple-element.21), channel_id=1, source_target_pairs={{0,2},{1,3},{2,0},{3,1},{4,6},{5,7},{6,4},{7,5},{8,10},{9,11},{10,... | collective-permute-start | bytes 393224 | tf_op jit(solution)/shard_map/ppermute | solution.py:29
  116.5 13.7 %collective-permute-start.28 = (bf16[64,1024]{1,0:T(8,128)(2,1)S(1)}, bf16[64,1024]{1,0:T(8,128)(2,1)S(1)}, u32[]{:S(2)}, u32[]{:S(2)}) collective-permute-start(bf16[64,1024]{1,0:T(8,128)(2,1)S(1)} %get-tuple-element.19), channel_id=1, source_target_pairs={{0,1},{1,0},{2,3},{3,2},{4,5},{5,4},{6,7},{7,6},{8,9},{9,8},{10,11... | collective-permute-start | bytes 393224 | tf_op jit(solution)/shard_map/ppermute | solution.py:29
  119.0 16.1 %collective-permute-start.15 = (bf16[320,1024]{1,0:T(8,128)(2,1)S(1)}, bf16[320,1024]{1,0:T(8,128)(2,1)S(1)}, u32[]{:S(2)}, u32[]{:S(2)}) collective-permute-start(bf16[320,1024]{1,0:T(8,128)(2,1)S(1)} %get-tuple-element.32), channel_id=1, source_target_pairs={{0,4},{4,0},{8,12},{12,8},{16,20},{20,16},{24,28},{28,24},{1,5},{5... | collective-permute-start | bytes 1966088 | tf_op jit(solution)/shard_map/ppermute | solution.py:29
  119.2 11.7 %collective-permute-start.20 = (bf16[32,1024]{1,0:T(8,128)(2,1)S(1)}, bf16[32,1024]{1,0:T(8,128)(2,1)S(1)}, u32[]{:S(2)}, u32[]{:S(2)}) collective-permute-start(bf16[32,1024]{1,0:T(8,128)(2,1)S(1)} %get-tuple-element.34), channel_id=1, source_target_pairs={{0,3},{1,2},{2,1},{3,0},{4,7},{5,6},{6,5},{7,4},{8,11},{9,10},{10,... | collective-permute-start | bytes 196616 | tf_op jit(solution)/shard_map/ppermute | solution.py:29
  122.4 9.2 %collective-permute-start.19 = (bf16[32,1024]{1,0:T(8,128)(2,1)S(1)}, bf16[32,1024]{1,0:T(8,128)(2,1)S(1)}, u32[]{:S(2)}, u32[]{:S(2)}) collective-permute-start(bf16[32,1024]{1,0:T(8,128)(2,1)S(1)} %get-tuple-element.35), channel_id=1, source_target_pairs={{0,2},{1,3},{2,0},{3,1},{4,6},{5,7},{6,4},{7,5},{8,10},{9,11},{10,... | collective-permute-start | bytes 196616 | tf_op jit(solution)/shard_map/ppermute | solution.py:29
  130.2 4.3 %collective-permute-start.18 = (bf16[32,1024]{1,0:T(8,128)(2,1)S(1)}, bf16[32,1024]{1,0:T(8,128)(2,1)S(1)}, u32[]{:S(2)}, u32[]{:S(2)}) collective-permute-start(bf16[32,1024]{1,0:T(8,128)(2,1)S(1)} %get-tuple-element.33), channel_id=1, source_target_pairs={{0,1},{1,0},{2,3},{3,2},{4,5},{5,4},{6,7},{7,6},{8,9},{9,8},{10,11... | collective-permute-start | bytes 196616 | tf_op jit(solution)/shard_map/ppermute | solution.py:29
  (15 other events, 37.2 us)

commit v2 on v1

v2 whole, which is shorter than its diff:
```python
import functools

import jax
import jax.numpy as jnp
from jax import lax
from jax.experimental import pallas as pl
from jax.experimental.pallas import tpu as pltpu
from jax.sharding import PartitionSpec as P

BF = jnp.bfloat16
F32 = jnp.float32
ROOM = 32 * 1024 * 1024


def inner(left, right):
    return lax.dot_general(
        left, right, (((0,), (0,)), ((), ())), preferred_element_type=F32
    )


def outer(left, right):
    return lax.dot_general(
        left, right, (((1,), (1,)), ((), ())), preferred_element_type=F32
    )


def times(left, right):
    return jnp.dot(left, right, preferred_element_type=F32)


def swap(value, axis, masks):
    count = lax.axis_size(axis)
    pairs = [(i, i ^ masks[i % len(masks)]) for i in range(count)]
    return lax.ppermute(value, axis, pairs)


def block_at(value, index, size, axis):
    return lax.dynamic_slice_in_dim(value, index * size, size, axis)


def like(rows, columns, kind):
    return jax.ShapeDtypeStruct((rows, columns), kind)


def run(body, outs, ins, after=(), numbers=None, scratch=(), flops=0):
    scalars = [] if numbers is None else [numbers]
    count, late = len(scalars) + len(ins), len(after)

    def kernel(*refs):
        body(*refs[:count], *refs[count + late :])

    moved = sum(a.size * a.dtype.itemsize for a in ins)
    return pl.pallas_call(
        kernel,
        out_shape=tuple(outs),
        in_specs=[pl.BlockSpec(memory_space=pltpu.SMEM)] * len(scalars)
        + [pl.BlockSpec(memory_space=pltpu.VMEM)] * len(ins)
        + [pl.BlockSpec(memory_space=pl.ANY)] * late,
        out_specs=tuple(pl.BlockSpec(memory_space=pltpu.VMEM) for _ in outs),
        scratch_shapes=list(scratch),
        compiler_params=pltpu.CompilerParams(vmem_limit_bytes=ROOM),
        cost_estimate=pl.CostEstimate(flops=flops, bytes_accessed=moved, transcendentals=0),
    )(*scalars, *ins, *after)


def sort_body(patch, part, own, numbers, grad, *blocks):
    size = own * part
    row = lax.broadcasted_iota(jnp.int32, (size, grad.shape[0]), 0)
    source = lax.broadcasted_iota(jnp.int32, (size, grad.shape[0]), 1)
    for m, block in enumerate(blocks):
        wanted = (row % part) * patch + numbers[m] * own + row // part
        block[...] = times((source == wanted).astype(BF), grad[...]).astype(BF)


def join_body(part, own, count, numbers, *refs):
    blocks, whole = refs[:-1], refs[-1]
    for m, block in enumerate(blocks):
        for j in range(own):
            start = pl.multiple_of((j * count + numbers[m]) * part, part)
            whole[pl.ds(start, part), :] = block[j * part : (j + 1) * part, :]


def product_body(shares, width, unit, places, moving, halves, numbers, *refs):
    left, rights = refs[0], refs[1 : 1 + halves]
    total = refs[-1]
    outs = refs[1 + halves : -1]
    kept, sent = outs[0], outs[1]
    count = len(places) // shares
    half = len(places) // 2
    if len(outs) == 3:
        first = 0
        for right in rights:
            outs[2][first : first + right.shape[0], :] = right[...]
            first += right.shape[0]
    for n in range(shares):
        if moving:
            start = pl.multiple_of(numbers[count + n] * width, width)
        else:
            start = n * width
        first = 0
        value = None
        for right in rights:
            rows = right.shape[0]
            term = inner(left[first : first + rows, pl.ds(start, width)], right[...])
            value = term if value is None else value + term
            first += rows
        total[...] = value
        for m in range(count):
            place = places[n * count + m]
            target = kept if place < half else sent
            row = (place % half) * unit
            block = total[pl.ds(pl.multiple_of(numbers[m] * unit, unit), unit), :]
            target[row : row + unit, :] = block.astype(target.dtype)


def add_body(kept, arrived, keep, send):
    half = keep.shape[0]
    keep[...] = (kept[:half, :].astype(F32) + arrived[:half, :].astype(F32)).astype(keep.dtype)
    send[...] = (kept[half:, :].astype(F32) + arrived[half:, :].astype(F32)).astype(send.dtype)


def sum_body(kept, arrived, whole):
    whole[...] = (kept[...].astype(F32) + arrived[...].astype(F32)).astype(whole.dtype)


def turned_body(kept, arrived, whole):
    whole[...] = (kept[...].astype(F32) + arrived[...].astype(F32)).T


def stack_body(first, second, both):
    rows = first.shape[0]
    both[:rows, :] = first[...]
    both[rows:, :] = second[...]


def on_device(
    byte_ids,
    global_out,
    global_in_grad,
    out_grad,
    proj_weight,
    emb_local,
    norm_gain,
    up_weight,
    down_weight,
):
    seq_count = lax.axis_size("seq")
    tp_count = lax.axis_size("tp")
    seq_place = lax.axis_index("seq")
    tp_place = lax.axis_index("tp")
    core = seq_place & 1
    chip = seq_place >> 1
    stages = seq_count.bit_length() - 2
    levels = tp_count.bit_length() - 1
    share_count = 1 << stages
    walks = (list(range(1, stages + 1)), list(range(stages, 0, -1)))
    patches, patch = byte_ids.shape
    slot, width = proj_weight.shape
    hidden = up_weight.shape[1]
    vocab = emb_local.shape[0]
    own = patch // tp_count
    part = patches // tp_count
    rows = own * patches

    def share_mask(number, walk):
        mask = 0
        for k in range(stages):
            if (number >> (stages - 1 - k)) & 1:
                mask |= 1 << (walk[k] - 1)
        return mask

    def shares_of(which):
        return [
            2 * (chip ^ jnp.where(which == 0, share_mask(n, walks[0]), share_mask(n, walks[1])))
            + which
            for n in range(share_count)
        ]

    shares = shares_of(core)
    others = shares_of(1 - core)
    near = [tp_place ^ m for m in range(tp_count)]
    numbers = jnp.stack(near + shares).astype(jnp.int32)

    def core_swap(value):
        return swap(value, "seq", (1,))

    def go(value, step):
        kind, k = step
        if kind == "seq":
            return swap(value, "seq", (1 << walks[0][k], 1 << walks[1][k]))
        return swap(value, "tp", (1 << k,))

    blocks = run(
        functools.partial(sort_body, patch, part, own),
        [like(own * part, width, BF)] * tp_count,
        [out_grad],
        numbers=numbers,
    )
    blocks = [swap(b, "tp", (m,)) if m else b for m, b in enumerate(blocks)]

    def by_slot(value):
        return [value[:, j * slot : (j + 1) * slot] for j in range(own)]

    slot_in = jnp.concatenate(by_slot(global_out) + by_slot(core_swap(global_out)), axis=0)
    ids = byte_ids.T
    ids = jnp.concatenate([ids, core_swap(ids)], axis=1)
    before = jnp.concatenate([jnp.full((1, 2 * patches), -1, jnp.int32), ids[:-1]], axis=0)

    def of_rows(value):
        mine = lax.dynamic_slice_in_dim(value, tp_place * own, own, 0)
        return jnp.swapaxes(mine.reshape(own, 2, patches), 0, 1).reshape(2 * rows)

    own_ids = of_rows(ids)[:rows]
    prev_ids = of_rows(before)
    prev_hot = (prev_ids[:, None] == jnp.arange(vocab)[None, :]).astype(BF)

    chunk = hidden // seq_count
    up_here = jnp.concatenate([block_at(up_weight, s, chunk, 1) for s in shares], axis=1)
    down_here = jnp.concatenate([block_at(down_weight, s, chunk, 0) for s in shares], axis=0)

    u_rows = times(slot_in, proj_weight) + times(prev_hot, emb_local)
    scale = lax.rsqrt(jnp.mean(u_rows * u_rows, axis=1, keepdims=True) + 1e-05)
    normed = u_rows * scale
    r_rows = (normed * norm_gain).astype(BF)
    a_rows = times(r_rows, up_here)
    sig = jax.nn.sigmoid(a_rows)
    h_rows = (a_rows * sig).astype(BF)

    height = vocab // seq_count

    def vocab_of(numbers):
        return jnp.concatenate([n * height + jnp.arange(height) for n in numbers])

    here, there = vocab_of(shares), vocab_of(others)
    gin = jnp.concatenate(by_slot(global_in_grad), axis=0)
    glob_sent = times((there[:, None] == own_ids[None, :]).astype(BF), gin).astype(BF)
    glob_kept = times((here[:, None] == own_ids[None, :]).astype(BF), gin)

    seq_steps = [("seq", k) for k in range(stages)]
    tp_steps = [("tp", k) for k in range(levels)]

    def add(kept, arrived, after):
        half = kept.shape[0] // 2
        kind = arrived.dtype
        outs = [like(half, kept.shape[1], kind)] * 2
        return run(add_body, outs, [kept, arrived], after)

    class Chain:
        def __init__(self, kept, sent, steps, turned):
            self.kept, self.steps, self.turned, self.at = kept, steps, turned, 0
            self.arrived = go(sent, steps[0])

        def next(self, after):
            self.at += 1
            if self.at < len(self.steps):
                self.kept, sent = add(self.kept, self.arrived, after)
                self.arrived = go(sent, self.steps[self.at])
                return self.kept
            if self.turned:
                shape = like(self.kept.shape[1], self.kept.shape[0], F32)
                (self.kept,) = run(turned_body, [shape], [self.kept, self.arrived], after)
            else:
                shape = like(self.kept.shape[0], self.kept.shape[1], F32)
                (self.kept,) = run(sum_body, [shape], [self.kept, self.arrived], after)
            return self.kept

    class Table:
        def __init__(self, kept, arrived):
            self.kept, self.arrived, self.at = kept, arrived, 0
            self.plan = (
                [("half", s) for s in seq_steps[1:]]
                + [("whole", s) for s in tp_steps]
                + [("join", s) for s in reversed(seq_steps)]
                + [("join", None)]
            )
            self.last = "half"

        def next(self, after):
            kind, step = self.plan[self.at] if self.at < len(self.plan) else ("end", None)
            rows, columns = self.kept.shape
            if self.last == "half" and kind == "half":
                self.kept, sent = add(self.kept, self.arrived, after)
            elif self.last == "join":
                shape = like(2 * rows, columns, BF)
                (self.kept,) = run(stack_body, [shape], [self.kept, self.arrived], after)
                sent = self.kept
            else:
                shape = like(rows, columns, BF)
                (self.kept,) = run(sum_body, [shape], [self.kept, self.arrived], after)
                sent = self.kept
            if kind != "end":
                self.arrived = core_swap(sent) if step is None else go(sent, step)
                self.last = kind
                self.at += 1
            return self.kept

    def product(left, rights, steps, moving, copied, after):
        share = left.shape[1] // share_count
        if moving:
            share = left.shape[1] // seq_count
            if share % 128:
                left = jnp.concatenate([block_at(left, s, share, 1) for s in shares], axis=1)
                moving = False
        unit = share // tp_count
        kind = BF if unit % 16 == 0 else F32
        places = []
        for n in range(share_count):
            for m in range(tp_count):
                place = 0
                for axis, k in steps:
                    digit = (n >> (stages - 1 - k)) & 1 if axis == "seq" else (m >> k) & 1
                    place = 2 * place + digit
                places.append(place)
        columns = rights[0].shape[1]
        height = share * share_count // 2
        outs = [like(height, columns, kind)] * 2
        if copied:
            outs.append(like(left.shape[0], columns, BF))
        body = functools.partial(
            product_body, share_count, share, unit, places, moving, len(rights)
        )
        return run(
            body,
            outs,
            [left, *rights],
            after,
            numbers=numbers,
            scratch=[pltpu.VMEM((share, columns), F32)],
            flops=4 * height * columns * left.shape[0],
        )

    glob_arrived = core_swap(glob_sent)
    half = glob_kept.shape[0] // 2
    glob_kept, glob_sent = add(glob_kept, glob_arrived, [h_rows])
    glob = Table(glob_kept, go(glob_sent, seq_steps[0]))
    (out_own,) = run(
        functools.partial(join_body, part, own, tp_count),
        [like(rows, width, BF)],
        blocks,
        [glob_kept, h_rows],
        numbers=numbers,
    )
    out_other = core_swap(out_own)
    last = glob.next([out_own])

    order = seq_steps + tp_steps
    kept, sent, out_rows = product(h_rows, [out_own, out_other], order, False, True, [last])
    down = Chain(kept, sent, order, False)
    dh_rows = outer(out_rows, down_here)
    da_rows = (dh_rows * sig * (1.0 + a_rows * (1.0 - sig))).astype(BF)
    dr_part = outer(da_rows, up_here)
    dr_sent = jnp.concatenate([dr_part[rows:], dr_part[:rows]], axis=0).astype(BF)
    dr_arrived = core_swap(dr_sent)
    last = glob.next([dr_sent])
    (dr_arrived,) = run(
        lambda a, b: b.__setitem__(Ellipsis, a[...]),
        [like(2 * rows, width, BF)],
        [dr_arrived],
        [last],
    )
    dr_rows = dr_part + dr_arrived.astype(F32)
    gain_part = jnp.sum(dr_rows * normed, axis=0)
    dn_rows = dr_rows * norm_gain
    du_rows = (
        out_rows.astype(F32)
        + scale * (dn_rows - normed * jnp.mean(dn_rows * normed, axis=1, keepdims=True))
    ).astype(BF)

    strip = width // seq_count
    emb_part = times((here[:, None] == prev_ids[None, :]).astype(BF), du_rows)
    lines = jnp.stack([block_at(gain_part, s, strip, 0) for s in shares])[:, None]
    lines = jnp.pad(lines, ((0, 0), (0, height - 1), (0, 0))).reshape(-1, strip)
    tables = jnp.concatenate([emb_part, lines], axis=1).astype(BF)
    half = tables.shape[0] // 2
    local_kept, local_sent = tables[:half], tables[half:]
    local = Table(local_kept, go(local_sent, seq_steps[0]))

    order = tp_steps[:1] + seq_steps + tp_steps[1:]
    kept, sent = product(du_rows, [slot_in], order, True, False, [local_sent])
    proj = Chain(kept, sent, order, True)
    order = seq_steps + tp_steps
    kept, sent = product(da_rows, [r_rows], order, False, False, [kept])
    up = Chain(kept, sent, order, True)
    back = outer(du_rows[:rows], proj_weight).astype(BF)
    glob_out_grad = jnp.concatenate(
        [back[j * patches : (j + 1) * patches] for j in range(own)], axis=1
    )

    last = kept
    seen = {down: 0, proj: 0, up: 0, local: 0, glob: 2}
    ends = {
        down: len(order),
        proj: len(order),
        up: len(order),
        local: len(local.plan) + 1,
        glob: len(glob.plan) + 1,
    }
    queue = [
        local, down, local, glob, proj, local, glob, down, local, up, proj, local,
        glob, down, proj, local, up, glob, local, down, proj, up, glob, up,
    ]
    for chain in queue + [local, proj, down, glob, up] * 16:
        if seen[chain] < ends[chain]:
            last = chain.next([last])
            seen[chain] += 1

    all_numbers = jnp.stack(shares + others)
    sort = jnp.arange(vocab)[:, None] == (
        all_numbers[:, None] * height + jnp.arange(height)[None, :]
    ).reshape(1, -1)
    sort = sort.astype(BF)
    emb_global_grad = times(sort, glob.kept)
    emb_local_grad = times(sort, local.kept[:, :width])
    gain_sort = (jnp.arange(seq_count)[:, None] == all_numbers[None, :]).astype(BF)
    gain_lines = local.kept[:, width:].reshape(seq_count, height, strip)[:, 0]
    gain_grad = times(gain_sort, gain_lines).reshape(width)
    return (
        glob_out_grad,
        emb_global_grad,
        emb_local_grad,
        gain_grad,
        proj.kept,
        up.kept,
        down.kept,
    )


def solution(mesh):
    placed = (
        P("seq", None),
        P("seq", "tp"),
        P("seq", "tp"),
        P(("seq", "tp"), None),
        P(),
        P(),
        P(),
        P(),
        P(),
    )
    return jax.shard_map(
        on_device,
        mesh=mesh,
        in_specs=placed,
        out_specs=(
            P("seq", "tp"),
            P(),
            P(),
            P(),
            P(None, ("seq", "tp")),
            P(None, ("seq", "tp")),
            P(("seq", "tp"), None),
        ),
        check_vma=False,
    )
```

time: 139 us -> 145 us (1.043)
  Pallas kernels: 0 us -> 21.6 us
  waiting for transfers between devices: 62.5 us -> 43.4 us
  local copies, waits for them, and re-layouts: 15 us -> 19.9 us
  other arithmetic: 5.84 us -> 4.31 us
    pallas_call x0 -> x33, Pallas kernels: none -> 21.6 us  [run(): pl.pallas_call(kernel, out_shape=tuple(outs), in_specs=[pl.BlockSpec(memo...]
    ppermute x31 -> x34, waiting for transfers between devices: 62.5 us -> 43.4 us  [swap(): return lax.ppermute(value, axis, pairs)]
    unnamed x42 -> x89, local copies, waits for them, and re-layouts: 1.88 us -> 11.6 us
    dot_general x6 -> x0, matrix products: 3.87 us -> none  [inner(): lax.dot_general(left, right, (((0,), (0,)), ((), ())), preferred_element_...]
    dot_general x3, matrix products: 4.11 us -> 7.54 us  [outer(): lax.dot_general(left, right, (((1,), (1,)), ((), ())), preferred_element_...]
    dynamic_slice x4 -> x2, local copies, waits for them, and re-layouts: 5.31 us -> 3.12 us  [block_at(): return lax.dynamic_slice_in_dim(value, index * size, size, axis)]
    dynamic_update_slice x4 -> x0, local copies, waits for them, and re-layouts: 1.87 us -> none  [on_device(): lax.dynamic_update_slice(out_own, block.reshape(own, 1, part, width), (0,...]
    transpose x2 -> x0, other arithmetic: 1.45 us -> none  [the longest x1 0.76 us: on_device(): up_grad = weight_sum(da_rows, r_rows).T]
  transfers between devices with their start and end apart: 31 -> 34, of which waited for: 12 -> 9; matrix products, arithmetic and copies ran while one was open for 20% -> 16% of each run, Pallas kernels for 0% -> 13%
where the time goes in v2:
time: 145 us; the launch traced here: 144 us
  waiting for transfers between devices  43.4 us (30%)
  starting transfers between devices  36.6 us (25%)
  Pallas kernels  21.6 us (15%)
  local copies, waits for them, and re-layouts  19.9 us (14%)
  matrix products  17 us (12%)
  other arithmetic  4.31 us (3%)
  between operations  1.52 us (1%)
    ppermute x34, waiting for transfers between devices, swap(): return lax.ppermute(value, axis, pairs)  43.4 us
    ppermute x34, starting transfers between devices, swap(): return lax.ppermute(value, axis, pairs)  36.6 us
    pallas_call x33, Pallas kernels, run(): pl.pallas_call(kernel, out_shape=tuple(outs), in_specs=[pl.BlockSpec(memo...  21.6 us
    unnamed x89, local copies, waits for them, and re-layouts  11.6 us
    dot_general x9, matrix products, times(): return jnp.dot(left, right, preferred_element_type=F32)  9.43 us
    dot_general x3, matrix products, outer(): lax.dot_general(left, right, (((1,), (1,)), ((), ())), preferred_element_...  7.54 us
    slice x3, local copies, waits for them, and re-layouts, by_slot(): return [value[:, j * slot:(j + 1) * slot] for j in range(own)]  4.68 us
    dynamic_slice x2, local copies, waits for them, and re-layouts, block_at(): return lax.dynamic_slice_in_dim(value, index * size, size, axis)  3.12 us
  transfers between devices with their start and end apart: 34, of which 9 were waited for; matrix products, arithmetic and copies ran while one was open for 16% of the time, Pallas kernels for 13%

profile of v2, /device:TPU:0, one launch (start us, length us, event | category | flops | bytes accessed | tf_op | source)
XLA Modules:
  0.0 144.2 jit_solution(8150777383280360125)
XLA Ops:
  3.4 3.1 %collective-permute-start.2 = (bf16[64,1024]{1,0:T(8,128)(2,1)S(1)}, bf16[64,1024]{1,0:T(8,128)(2,1)S(1)}, u32[]{:S(2)}, u32[]{:S(2)}) collective-permute-start(bf16[64,1024]{1,0:T(8,128)(2,1)S(1)} %get-tuple-element.43), channel_id=1, source_target_pairs={{0,1},{1,0},{2,3},{3,2},{4,5},{5,4},{6,7},{7,6},{8,9},{9,8},{10,11... | collective-permute-start | bytes 393224 | tf_op jit(solution)/shard_map/ppermute | solution.py:34
  6.5 2.6 %collective-permute-start.3 = (bf16[64,1024]{1,0:T(8,128)(2,1)S(1)}, bf16[64,1024]{1,0:T(8,128)(2,1)S(1)}, u32[]{:S(2)}, u32[]{:S(2)}) collective-permute-start(bf16[64,1024]{1,0:T(8,128)(2,1)S(1)} %get-tuple-element.44), channel_id=1, source_target_pairs={{0,2},{1,3},{2,0},{3,1},{4,6},{5,7},{6,4},{7,5},{8,10},{9,11},{10,... | collective-permute-start | bytes 393224 | tf_op jit(solution)/shard_map/ppermute | solution.py:34
  9.1 1.9 %fusion.42 = (bf16[128,1024]{1,0:T(8,128)(2,1)}, bf16[128,1024]{1,0:T(8,128)(2,1)}) fusion(bf16[128,2048]{1,0:T(8,128)(2,1)} %param.10), kind=kLoop, calls=%fused_computation.98 | loop fusion | bytes 1048576 | tf_op jit(solution)/shard_map/slice | solution.py:202
  10.9 1.8 %fusion.41 = (bf16[128,1024]{1,0:T(8,128)(2,1)S(1)}, bf16[128,1024]{1,0:T(8,128)(2,1)}) fusion(bf16[128,2048]{1,0:T(8,128)(2,1)} %param.11), kind=kLoop, calls=%fused_computation.97 | loop fusion | bytes 1048576 | tf_op jit(solution)/shard_map/slice | solution.py:202
  12.8 2.9 %constant_dynamic-slice_fusion.7 = (bf16[1024,256]{1,0:T(8,128)(2,1)}, bf16[1024,256]{1,0:T(8,128)(2,1)}, bf16[1024,256]{1,0:T(8,128)(2,1)}, bf16[1024,256]{1,0:T(8,128)(2,1)}) fusion(bf16[1024,2048]{1,0:T(8,128)(2,1)} %param.16, s32[]{:T(128)S(6)} %select_n.52, s32[]{:T(128)S(6)} %select_n.53, s32[]{:T(128)S(6)} %select_n.55, s32[]{:T(128)S(6)} %select_n.54), kind=kLoop, calls=%fused_computation.68 | loop fusion | bytes 4194320 | tf_op jit(solution)/shard_map/dynamic_slice | solution.py:38
  20.1 1.4 multiply_reduce_fusion.2
  24.1 1.5 %multiply_convert_fusion.1 = (bf16[512,1024]{1,0:T(8,128)(2,1)S(1)}, f32[512,1024]{1,0:T(8,128)S(1)}) fusion(bf16[512,1024]{1,0:T(8,128)(2,1)S(1)} %multiply_convert_fusion.2.refs_2_, bf16[1024,256]{1,0:T(8,128)(2,1)S(1)} %copy-done.35, bf16[1024,256]{1,0:T(8,128)(2,1)S(1)} %copy-done.36, bf16[1024,256]{1,0:T(8,128)(2,1)S(1)} %copy-done.34, ...), kind=kOutput, calls=%fused_computation.14 | convolution fusion | flops 1084751872 | bytes 6291456 | tf_op jit(solution)/shard_map/dot_general | solution.py:28
  26.9 1.7 %collective-permute-start.7 = (bf16[64,1024]{1,0:T(8,128)(2,1)S(1)}, bf16[64,1024]{1,0:T(8,128)(2,1)S(1)}, u32[]{:S(2)}, u32[]{:S(2)}) collective-permute-start(bf16[64,1024]{1,0:T(8,128)(2,1)S(1)} %get-tuple-element.47), channel_id=1, source_target_pairs={{0,8},{4,20},{8,0},{12,28},{16,24},{20,4},{24,16},{28,12},{1,9},{5... | collective-permute-start | bytes 393224 | tf_op jit(solution)/shard_map/ppermute | solution.py:34
  28.8 3.0 %collective-permute-done.7.refs_1_ = bf16[64,1024]{1,0:T(8,128)(2,1)S(1)} collective-permute-done((bf16[64,1024]{1,0:T(8,128)(2,1)S(1)}, bf16[64,1024]{1,0:T(8,128)(2,1)S(1)}, u32[]{:S(2)}, u32[]{:S(2)}) %collective-permute-start.7) | collective-permute-done | bytes 131104 | tf_op jit(solution)/shard_map/ppermute | solution.py:34
  31.9 2.0 %shard_map.148 = (bf16[512,1024]{1,0:T(8,128)(2,1)S(1)}, bf16[512,1024]{1,0:T(8,128)(2,1)S(1)}, bf16[512,1024]{1,0:T(8,128)(2,1)S(1)}) custom-call(s32[8]{0:T(128)S(1)} %stack.74.refs_0_, bf16[512,1024]{1,0:T(8,128)(2,1)S(1)} %get-tuple-element.119.refs_2_.refs_6_.refs_1_, bf16[256,1024]{1,0:T(8,128)(2,1)S(1)} %shard_map.146.refs_2_, ...), custom_call_target="tpu_custom_call" | custom-call | flops 1073741824 | bytes 2097152 | tf_op jit(solution)/shard_map/pallas_call | solution.py:53
  33.9 4.2 %multiply_convert_fusion.refs_1_ = bf16[512,1024]{1,0:T(8,128)(2,1)S(1)} fusion(f32[512,1024]{1,0:T(8,128)S(1)} %get-tuple-element.120, bf16[512,1024]{1,0:T(8,128)(2,1)S(1)} %get-tuple-element.49, bf16[256,1024]{1,0:T(8,128)(2,1)S(1)} %get-tuple-element.95, bf16[256,1024]{1,0:T(8,128)(2,1)S(1)} %get-tuple-element.96, ...), kind=kOutput, calls=%fused_computation.13 | convolution fusion | flops 1086849024 | bytes 6291456 | tf_op jit(solution)/shard_map/dot_general | solution.py:22
  38.1 2.6 %fusion.44 = (bf16[512,1024]{1,0:T(8,128)(2,1)S(1)}, f32[512,1024]{1,0:T(8,128)}) fusion(bf16[512,1024]{1,0:T(8,128)(2,1)S(1)} %multiply_convert_fusion.refs_1_, bf16[1024,256]{1,0:T(8,128)(2,1)S(1)} %copy-done.35, bf16[1024,256]{1,0:T(8,128)(2,1)S(1)} %copy-done.36, bf16[1024,256]{1,0:T(8,128)(2,1)S(1)} %copy-done.34, bf16[1024,256]{1,0:T(8,128)(2,1)S(1)} %copy-done.33), kind=kOutput, calls=%fused_computation.100 | convolution fusion | flops 1082654720 | bytes 6291456 | tf_op jit(solution)/shard_map/dot_general | solution.py:22
  41.0 1.8 %collective-permute-start.9 = (bf16[32,1024]{1,0:T(8,128)(2,1)S(1)}, bf16[32,1024]{1,0:T(8,128)(2,1)S(1)}, u32[]{:S(2)}, u32[]{:S(2)}) collective-permute-start(bf16[32,1024]{1,0:T(8,128)(2,1)S(1)} %get-tuple-element.50), channel_id=1, source_target_pairs={{0,16},{4,12},{8,24},{12,4},{16,0},{20,28},{24,8},{28,20},{1,17},{... | collective-permute-start | bytes 196616 | tf_op jit(solution)/shard_map/ppermute | solution.py:34
  42.8 1.3 pad_maximum_fusion.1.refs_2_
  44.2 1.6 %collective-permute-start.13 = (bf16[512,1024]{1,0:T(8,128)(2,1)S(1)}, bf16[512,1024]{1,0:T(8,128)(2,1)S(1)}, u32[]{:S(2)}, u32[]{:S(2)}) collective-permute-start(bf16[512,1024]{1,0:T(8,128)(2,1)S(1)} %copy-done.20), channel_id=1, source_target_pairs={{0,8},{4,20},{8,0},{12,28},{16,24},{20,4},{24,16},{28,12},{1,9},{5... | collective-permute-start | bytes 3145736 | tf_op jit(solution)/shard_map/ppermute | solution.py:34
  49.6 2.1 %shard_map.151 = (bf16[256,1024]{1,0:T(8,128)(2,1)S(1)}, bf16[256,1024]{1,0:T(8,128)(2,1)}) custom-call(s32[8]{0:T(128)S(1)} %stack.74.refs_0_, bf16[512,1024]{1,0:T(8,128)(2,1)S(1)} %add_convert_fusion.refs_1_, bf16[512,1024]{1,0:T(8,128)(2,1)S(1)} %pad_maximum_fusion.1.refs_2_, bf16[64,1152]{1,0:T(8,128)(2,1)S(1)} %get-tuple-element.111.refs_3_), custom_call_target="tpu_custom_call" | custom-call | flops 536870912 | bytes 2097152 | tf_op jit(solution)/shard_map/pallas_call | solution.py:53
  51.7 2.9 %shard_map.152 = (bf16[512,1024]{1,0:T(8,128)(2,1)S(1)}, bf16[512,1024]{1,0:T(8,128)(2,1)}) custom-call(s32[8]{0:T(128)S(1)} %stack.74.refs_0_, bf16[512,1024]{1,0:T(8,128)(2,1)S(1)} %copy-done.23, bf16[512,1024]{1,0:T(8,128)(2,1)S(1)} %copy-done.7, bf16[256,1024]{1,0:T(8,128)(2,1)S(1)} %get-tuple-element.51.refs_3_.refs_0_), custom_call_target="tpu_custom_call" | custom-call | flops 1073741824 | bytes 2097152 | tf_op jit(solution)/shard_map/pallas_call | solution.py:53
  57.3 14.5 %collective-permute-done.11.refs_1_ = bf16[64,1152]{1,0:T(8,128)(2,1)S(1)} collective-permute-done((bf16[64,1152]{1,0:T(8,128)(2,1)S(1)}, bf16[64,1152]{1,0:T(8,128)(2,1)S(1)}, u32[]{:S(2)}, u32[]{:S(2)}) %collective-permute-start.11) | collective-permute-done | bytes 147488 | tf_op jit(solution)/shard_map/ppermute | solution.py:34
  75.9 8.2 %collective-permute-done.12.refs_1_ = bf16[32,1152]{1,0:T(8,128)(2,1)S(1)} collective-permute-done((bf16[32,1152]{1,0:T(8,128)(2,1)S(1)}, bf16[32,1152]{1,0:T(8,128)(2,1)S(1)}, u32[]{:S(2)}, u32[]{:S(2)}) %collective-permute-start.12) | collective-permute-done | bytes 73760 | tf_op jit(solution)/shard_map/ppermute | solution.py:34
  85.5 1.3 collective-permute-start.10
  87.0 2.9 %collective-permute-done.10.refs_1_ = bf16[32,1024]{1,0:T(8,128)(2,1)S(1)} collective-permute-done((bf16[32,1024]{1,0:T(8,128)(2,1)S(1)}, bf16[32,1024]{1,0:T(8,128)(2,1)S(1)}, u32[]{:S(2)}, u32[]{:S(2)}) %collective-permute-start.10) | collective-permute-done | bytes 65568 | tf_op jit(solution)/shard_map/ppermute | solution.py:34
  89.9 3.9 %collective-permute-start.14 = (bf16[32,1024]{1,0:T(8,128)(2,1)S(1)}, bf16[32,1024]{1,0:T(8,128)(2,1)S(1)}, u32[]{:S(2)}, u32[]{:S(2)}) collective-permute-start(bf16[32,1024]{1,0:T(8,128)(2,1)S(1)} %shard_map.156.refs_2_.refs_0_), channel_id=1, source_target_pairs={{0,2},{1,3},{2,0},{3,1},{4,6},{5,7},{6,4},{7,5},{8,10},{9,11},{10,... | collective-permute-start | bytes 196616 | tf_op jit(solution)/shard_map/ppermute | solution.py:34
  94.9 1.8 %shard_map.157 = (bf16[128,1024]{1,0:T(8,128)(2,1)S(1)}, bf16[128,1024]{1,0:T(8,128)(2,1)}) custom-call(bf16[256,1024]{1,0:T(8,128)(2,1)S(1)} %copy-done.18, bf16[256,1024]{1,0:T(8,128)(2,1)} %collective-permute-done.16.refs_1_, bf16[32,1024]{1,0:T(8,128)(2,1)S(1)} %shard_map.156.refs_2_.refs_0_), custom_call_target="tpu_custom_call" | custom-call | bytes 1048576 | tf_op jit(solution)/shard_map/pallas_call | solution.py:53
  99.1 3.4 %collective-permute-done.18.refs_1_ = bf16[32,1152]{1,0:T(8,128)(2,1)S(1)} collective-permute-done((bf16[32,1152]{1,0:T(8,128)(2,1)S(1)}, bf16[32,1152]{1,0:T(8,128)(2,1)S(1)}, u32[]{:S(2)}, u32[]{:S(2)}) %collective-permute-start.18) | collective-permute-done | bytes 73760 | tf_op jit(solution)/shard_map/ppermute | solution.py:34
  106.1 1.5 %shard_map.162 = (bf16[256,1024]{1,0:T(8,128)(2,1)S(1)}, bf16[256,1024]{1,0:T(8,128)(2,1)S(1)}) custom-call(bf16[512,1024]{1,0:T(8,128)(2,1)S(1)} %copy-done.2, bf16[512,1024]{1,0:T(8,128)(2,1)} %collective-permute-done.22.refs_1_, bf16[32,1152]{1,0:T(8,128)(2,1)S(1)} %shard_map.161.refs_2_.refs_0_), custom_call_target="tpu_custom_call" | custom-call | bytes 2097152 | tf_op jit(solution)/shard_map/pallas_call | solution.py:53
  110.4 1.6 %collective-permute-start.25 = (bf16[64,1152]{1,0:T(8,128)(2,1)S(1)}, bf16[64,1152]{1,0:T(8,128)(2,1)S(1)}, u32[]{:S(2)}, u32[]{:S(2)}) collective-permute-start(bf16[64,1152]{1,0:T(8,128)(2,1)S(1)} %shard_map.164.refs_2_.refs_0_), channel_id=1, source_target_pairs={{0,8},{4,20},{8,0},{12,28},{16,24},{20,4},{24,16},{28,12},{1,9},{5... | collective-permute-start | bytes 442376 | tf_op jit(solution)/shard_map/ppermute | solution.py:34
  114.0 2.2 %collective-permute-done.25.refs_1_ = bf16[64,1152]{1,0:T(8,128)(2,1)S(1)} collective-permute-done((bf16[64,1152]{1,0:T(8,128)(2,1)S(1)}, bf16[64,1152]{1,0:T(8,128)(2,1)S(1)}, u32[]{:S(2)}, u32[]{:S(2)}) %collective-permute-start.25) | collective-permute-done | bytes 147488 | tf_op jit(solution)/shard_map/ppermute | solution.py:34
  116.3 1.7 %collective-permute-start.23 = (bf16[64,1024]{1,0:T(8,128)(2,1)S(1)}, bf16[64,1024]{1,0:T(8,128)(2,1)S(1)}, u32[]{:S(2)}, u32[]{:S(2)}) collective-permute-start(bf16[64,1024]{1,0:T(8,128)(2,1)S(1)} %shard_map.165.refs_2_.refs_0_), channel_id=1, source_target_pairs={{0,8},{4,20},{8,0},{12,28},{16,24},{20,4},{24,16},{28,12},{1,9},{5... | collective-permute-start | bytes 393224 | tf_op jit(solution)/shard_map/ppermute | solution.py:34
  118.9 2.0 %collective-permute-start.30 = (bf16[32,1024]{1,0:T(8,128)(2,1)S(1)}, bf16[32,1024]{1,0:T(8,128)(2,1)S(1)}, u32[]{:S(2)}, u32[]{:S(2)}) collective-permute-start(bf16[32,1024]{1,0:T(8,128)(2,1)S(1)} %get-tuple-element.73), channel_id=1, source_target_pairs={{0,2},{1,3},{2,0},{3,1},{4,6},{5,7},{6,4},{7,5},{8,10},{9,11},{10,... | collective-permute-start | bytes 196616 | tf_op jit(solution)/shard_map/ppermute | solution.py:34
  123.3 2.0 %collective-permute-start.29 = (bf16[128,1024]{1,0:T(8,128)(2,1)}, bf16[128,1024]{1,0:T(8,128)(2,1)}, u32[]{:S(2)}, u32[]{:S(2)}) collective-permute-start(bf16[128,1024]{1,0:T(8,128)(2,1)} %get-tuple-element.72), channel_id=1, source_target_pairs={{0,1},{1,0},{2,3},{3,2},{4,5},{5,4},{6,7},{7,6},{8,9},{9,8},{10,11... | collective-permute-start | bytes 786440 | tf_op jit(solution)/shard_map/ppermute | solution.py:34
  125.5 3.3 %collective-permute-done.31.refs_1_ = bf16[64,1024]{1,0:T(8,128)(2,1)S(1)} collective-permute-done((bf16[64,1024]{1,0:T(8,128)(2,1)S(1)}, bf16[64,1024]{1,0:T(8,128)(2,1)S(1)}, u32[]{:S(2)}, u32[]{:S(2)}) %collective-permute-start.31) | collective-permute-done | bytes 131104 | tf_op jit(solution)/shard_map/ppermute | solution.py:34
  138.1 5.1 %collective-permute-done.33.refs_1_ = bf16[64,1024]{1,0:T(8,128)(2,1)S(1)} collective-permute-done((bf16[64,1024]{1,0:T(8,128)(2,1)S(1)}, bf16[64,1024]{1,0:T(8,128)(2,1)S(1)}, u32[]{:S(2)}, u32[]{:S(2)}) %collective-permute-start.33) | collective-permute-done | bytes 131104 | tf_op jit(solution)/shard_map/ppermute | solution.py:34
  (206 shorter events, 49.0 us)
Async XLA Ops:
  0.6 15.1 %collective-permute-start.1 = (s32[8,128]{1,0:T(8,128)}, s32[8,128]{1,0:T(8,128)S(1)}, u32[]{:S(2)}, u32[]{:S(2)}) collective-permute-start(s32[8,128]{1,0:T(8,128)} %bitcast.49), channel_id=1, source_target_pairs={{0,4},{4,0},{8,12},{12,8},{16,20},{20,16},{24,28},{28,24},{1,5},{5... | collective-permute-start | bytes 12296 | tf_op jit(solution)/shard_map/ppermute | solution.py:34
  1.2 17.8 %collective-permute-start = (bf16[128,2048]{1,0:T(8,128)(2,1)}, bf16[128,2048]{1,0:T(8,128)(2,1)}, u32[]{:S(2)}, u32[]{:S(2)}) collective-permute-start(bf16[128,2048]{1,0:T(8,128)(2,1)} %param.10), channel_id=1, source_target_pairs={{0,4},{4,0},{8,12},{12,8},{16,20},{20,16},{24,28},{28,24},{1,5},{5... | collective-permute-start | bytes 1572872 | tf_op jit(solution)/shard_map/ppermute | solution.py:34
  3.4 22.3 %collective-permute-start.2 = (bf16[64,1024]{1,0:T(8,128)(2,1)S(1)}, bf16[64,1024]{1,0:T(8,128)(2,1)S(1)}, u32[]{:S(2)}, u32[]{:S(2)}) collective-permute-start(bf16[64,1024]{1,0:T(8,128)(2,1)S(1)} %get-tuple-element.43), channel_id=1, source_target_pairs={{0,1},{1,0},{2,3},{3,2},{4,5},{5,4},{6,7},{7,6},{8,9},{9,8},{10,11... | collective-permute-start | bytes 393224 | tf_op jit(solution)/shard_map/ppermute | solution.py:34
  6.5 19.3 %collective-permute-start.3 = (bf16[64,1024]{1,0:T(8,128)(2,1)S(1)}, bf16[64,1024]{1,0:T(8,128)(2,1)S(1)}, u32[]{:S(2)}, u32[]{:S(2)}) collective-permute-start(bf16[64,1024]{1,0:T(8,128)(2,1)S(1)} %get-tuple-element.44), channel_id=1, source_target_pairs={{0,2},{1,3},{2,0},{3,1},{4,6},{5,7},{6,4},{7,5},{8,10},{9,11},{10,... | collective-permute-start | bytes 393224 | tf_op jit(solution)/shard_map/ppermute | solution.py:34
  9.1 16.7 %collective-permute-start.4 = (bf16[64,1024]{1,0:T(8,128)(2,1)S(1)}, bf16[64,1024]{1,0:T(8,128)(2,1)S(1)}, u32[]{:S(2)}, u32[]{:S(2)}) collective-permute-start(bf16[64,1024]{1,0:T(8,128)(2,1)S(1)} %get-tuple-element.45), channel_id=1, source_target_pairs={{0,3},{1,2},{2,1},{3,0},{4,7},{5,6},{6,5},{7,4},{8,11},{9,10},{10,... | collective-permute-start | bytes 393224 | tf_op jit(solution)/shard_map/ppermute | solution.py:34
  17.1 8.5 %collective-permute-start.5 = (bf16[128,1024]{1,0:T(8,128)(2,1)S(1)}, bf16[128,1024]{1,0:T(8,128)(2,1)S(1)}, u32[]{:S(2)}, u32[]{:S(2)}) collective-permute-start(bf16[128,1024]{1,0:T(8,128)(2,1)S(1)} %convolution_convert_fusion.1), channel_id=1, source_target_pairs={{0,4},{4,0},{8,12},{12,8},{16,20},{20,16},{24,28},{28,24},{1,5},{5... | collective-permute-start | bytes 786440 | tf_op jit(solution)/shard_map/ppermute | solution.py:34
  26.3 5.6 %collective-permute-start.6 = (bf16[256,1024]{1,0:T(8,128)(2,1)S(1)}, bf16[256,1024]{1,0:T(8,128)(2,1)S(1)}, u32[]{:S(2)}, u32[]{:S(2)}) collective-permute-start(bf16[256,1024]{1,0:T(8,128)(2,1)S(1)} %shard_map.146.refs_2_), channel_id=1, source_target_pairs={{0,4},{4,0},{8,12},{12,8},{16,20},{20,16},{24,28},{28,24},{1,5},{5... | collective-permute-start | bytes 1572872 | tf_op jit(solution)/shard_map/ppermute | solution.py:34
  26.9 5.0 %collective-permute-start.7 = (bf16[64,1024]{1,0:T(8,128)(2,1)S(1)}, bf16[64,1024]{1,0:T(8,128)(2,1)S(1)}, u32[]{:S(2)}, u32[]{:S(2)}) collective-permute-start(bf16[64,1024]{1,0:T(8,128)(2,1)S(1)} %get-tuple-element.47), channel_id=1, source_target_pairs={{0,8},{4,20},{8,0},{12,28},{16,24},{20,4},{24,16},{28,12},{1,9},{5... | collective-permute-start | bytes 393224 | tf_op jit(solution)/shard_map/ppermute | solution.py:34
  40.9 4.9 %collective-permute-start.8 = (bf16[512,1024]{1,0:T(8,128)(2,1)S(1)}, bf16[512,1024]{1,0:T(8,128)(2,1)}, u32[]{:S(2)}, u32[]{:S(2)}) collective-permute-start(bf16[512,1024]{1,0:T(8,128)(2,1)S(1)} %pad_maximum_fusion.2.refs_2_), channel_id=1, source_target_pairs={{0,4},{4,0},{8,12},{12,8},{16,20},{20,16},{24,28},{28,24},{1,5},{5... | collective-permute-start | bytes 3145736 | tf_op jit(solution)/shard_map/ppermute | solution.py:34
  44.2 28.7 %collective-permute-start.13 = (bf16[512,1024]{1,0:T(8,128)(2,1)S(1)}, bf16[512,1024]{1,0:T(8,128)(2,1)S(1)}, u32[]{:S(2)}, u32[]{:S(2)}) collective-permute-start(bf16[512,1024]{1,0:T(8,128)(2,1)S(1)} %copy-done.20), channel_id=1, source_target_pairs={{0,8},{4,20},{8,0},{12,28},{16,24},{20,4},{24,16},{28,12},{1,9},{5... | collective-permute-start | bytes 3145736 | tf_op jit(solution)/shard_map/ppermute | solution.py:34
  54.6 50.2 %collective-permute-start.22 = (bf16[512,1024]{1,0:T(8,128)(2,1)}, bf16[512,1024]{1,0:T(8,128)(2,1)}, u32[]{:S(2)}, u32[]{:S(2)}) collective-permute-start(bf16[512,1024]{1,0:T(8,128)(2,1)} %get-tuple-element.63), channel_id=1, source_target_pairs={{0,8},{4,20},{8,0},{12,28},{16,24},{20,4},{24,16},{28,12},{1,9},{5... | collective-permute-start | bytes 3145736 | tf_op jit(solution)/shard_map/ppermute | solution.py:34
  56.0 37.9 %collective-permute-start.16 = (bf16[256,1024]{1,0:T(8,128)(2,1)}, bf16[256,1024]{1,0:T(8,128)(2,1)}, u32[]{:S(2)}, u32[]{:S(2)}) collective-permute-start(bf16[256,1024]{1,0:T(8,128)(2,1)} %get-tuple-element.58), channel_id=1, source_target_pairs={{0,1},{1,0},{2,3},{3,2},{4,5},{5,4},{6,7},{7,6},{8,9},{9,8},{10,11... | collective-permute-start | bytes 1572872 | tf_op jit(solution)/shard_map/ppermute | solution.py:34
  56.7 15.2 %collective-permute-start.11 = (bf16[64,1152]{1,0:T(8,128)(2,1)S(1)}, bf16[64,1152]{1,0:T(8,128)(2,1)S(1)}, u32[]{:S(2)}, u32[]{:S(2)}) collective-permute-start(bf16[64,1152]{1,0:T(8,128)(2,1)S(1)} %get-tuple-element.111.refs_3_), channel_id=1, source_target_pairs={{0,8},{4,20},{8,0},{12,28},{16,24},{20,4},{24,16},{28,12},{1,9},{5... | collective-permute-start | bytes 442376 | tf_op jit(solution)/shard_map/ppermute | solution.py:34
  73.8 24.1 %collective-permute-start.19 = (bf16[256,1024]{1,0:T(8,128)(2,1)}, bf16[256,1024]{1,0:T(8,128)(2,1)}, u32[]{:S(2)}, u32[]{:S(2)}) collective-permute-start(bf16[256,1024]{1,0:T(8,128)(2,1)} %get-tuple-element.60), channel_id=1, source_target_pairs={{0,16},{4,12},{8,24},{12,4},{16,0},{20,28},{24,8},{28,20},{1,17},{... | collective-permute-start | bytes 1572872 | tf_op jit(solution)/shard_map/ppermute | solution.py:34
  74.6 9.4 %collective-permute-start.12 = (bf16[32,1152]{1,0:T(8,128)(2,1)S(1)}, bf16[32,1152]{1,0:T(8,128)(2,1)S(1)}, u32[]{:S(2)}, u32[]{:S(2)}) collective-permute-start(bf16[32,1152]{1,0:T(8,128)(2,1)S(1)} %get-tuple-element.54), channel_id=1, source_target_pairs={{0,16},{4,12},{8,24},{12,4},{16,0},{20,28},{24,8},{28,20},{1,17},{... | collective-permute-start | bytes 221192 | tf_op jit(solution)/shard_map/ppermute | solution.py:34
  84.9 11.8 %collective-permute-start.15 = (bf16[32,1152]{1,0:T(8,128)(2,1)S(1)}, bf16[32,1152]{1,0:T(8,128)(2,1)S(1)}, u32[]{:S(2)}, u32[]{:S(2)}) collective-permute-start(bf16[32,1152]{1,0:T(8,128)(2,1)S(1)} %shard_map.155.refs_2_.refs_0_), channel_id=1, source_target_pairs={{0,1},{1,0},{2,3},{3,2},{4,5},{5,4},{6,7},{7,6},{8,9},{9,8},{10,11... | collective-permute-start | bytes 221192 | tf_op jit(solution)/shard_map/ppermute | solution.py:34
  89.9 8.0 %collective-permute-start.14 = (bf16[32,1024]{1,0:T(8,128)(2,1)S(1)}, bf16[32,1024]{1,0:T(8,128)(2,1)S(1)}, u32[]{:S(2)}, u32[]{:S(2)}) collective-permute-start(bf16[32,1024]{1,0:T(8,128)(2,1)S(1)} %shard_map.156.refs_2_.refs_0_), channel_id=1, source_target_pairs={{0,2},{1,3},{2,0},{3,1},{4,6},{5,7},{6,4},{7,5},{8,10},{9,11},{10,... | collective-permute-start | bytes 196616 | tf_op jit(solution)/shard_map/ppermute | solution.py:34
  96.7 5.9 %collective-permute-start.18 = (bf16[32,1152]{1,0:T(8,128)(2,1)S(1)}, bf16[32,1152]{1,0:T(8,128)(2,1)S(1)}, u32[]{:S(2)}, u32[]{:S(2)}) collective-permute-start(bf16[32,1152]{1,0:T(8,128)(2,1)S(1)} %shard_map.158.refs_2_.refs_0_), channel_id=1, source_target_pairs={{0,2},{1,3},{2,0},{3,1},{4,6},{5,7},{6,4},{7,5},{8,10},{9,11},{10,... | collective-permute-start | bytes 221192 | tf_op jit(solution)/shard_map/ppermute | solution.py:34
  96.8 10.8 %collective-permute-start.21 = (bf16[128,1024]{1,0:T(8,128)(2,1)}, bf16[128,1024]{1,0:T(8,128)(2,1)}, u32[]{:S(2)}, u32[]{:S(2)}) collective-permute-start(bf16[128,1024]{1,0:T(8,128)(2,1)} %get-tuple-element.62), channel_id=1, source_target_pairs={{0,8},{4,20},{8,0},{12,28},{16,24},{20,4},{24,16},{28,12},{1,9},{5... | collective-permute-start | bytes 786440 | tf_op jit(solution)/shard_map/ppermute | solution.py:34
  102.6 6.8 %collective-permute-start.20 = (bf16[32,1152]{1,0:T(8,128)(2,1)S(1)}, bf16[32,1152]{1,0:T(8,128)(2,1)}, u32[]{:S(2)}, u32[]{:S(2)}) collective-permute-start(bf16[32,1152]{1,0:T(8,128)(2,1)S(1)} %shard_map.161.refs_2_.refs_0_), channel_id=1, source_target_pairs={{0,16},{4,12},{8,24},{12,4},{16,0},{20,28},{24,8},{28,20},{1,17},{... | collective-permute-start | bytes 221192 | tf_op jit(solution)/shard_map/ppermute | solution.py:34
  103.6 10.3 %collective-permute-start.17 = (bf16[32,1024]{1,0:T(8,128)(2,1)S(1)}, bf16[32,1024]{1,0:T(8,128)(2,1)S(1)}, u32[]{:S(2)}, u32[]{:S(2)}) collective-permute-start(bf16[32,1024]{1,0:T(8,128)(2,1)S(1)} %shard_map.159.refs_2_.refs_0_), channel_id=1, source_target_pairs={{0,16},{4,12},{8,24},{12,4},{16,0},{20,28},{24,8},{28,20},{1,17},{... | collective-permute-start | bytes 196616 | tf_op jit(solution)/shard_map/ppermute | solution.py:34
  104.9 9.0 %collective-permute-start.27 = (bf16[128,1024]{1,0:T(8,128)(2,1)}, bf16[128,1024]{1,0:T(8,128)(2,1)S(1)}, u32[]{:S(2)}, u32[]{:S(2)}) collective-permute-start(bf16[128,1024]{1,0:T(8,128)(2,1)} %copy-done.21), channel_id=1, source_target_pairs={{0,1},{1,0},{2,3},{3,2},{4,5},{5,4},{6,7},{7,6},{8,9},{9,8},{10,11... | collective-permute-start | bytes 786440 | tf_op jit(solution)/shard_map/ppermute | solution.py:34
  108.6 5.3 %collective-permute-start.26 = (bf16[64,1024]{1,0:T(8,128)(2,1)S(1)}, bf16[64,1024]{1,0:T(8,128)(2,1)S(1)}, u32[]{:S(2)}, u32[]{:S(2)}) collective-permute-start(bf16[64,1024]{1,0:T(8,128)(2,1)S(1)} %get-tuple-element.67), channel_id=1, source_target_pairs={{0,16},{4,12},{8,24},{12,4},{16,0},{20,28},{24,8},{28,20},{1,17},{... | collective-permute-start | bytes 393224 | tf_op jit(solution)/shard_map/ppermute | solution.py:34
  110.4 5.8 %collective-permute-start.25 = (bf16[64,1152]{1,0:T(8,128)(2,1)S(1)}, bf16[64,1152]{1,0:T(8,128)(2,1)S(1)}, u32[]{:S(2)}, u32[]{:S(2)}) collective-permute-start(bf16[64,1152]{1,0:T(8,128)(2,1)S(1)} %shard_map.164.refs_2_.refs_0_), channel_id=1, source_target_pairs={{0,8},{4,20},{8,0},{12,28},{16,24},{20,4},{24,16},{28,12},{1,9},{5... | collective-permute-start | bytes 442376 | tf_op jit(solution)/shard_map/ppermute | solution.py:34
  111.9 10.6 %collective-permute-start.24 = (bf16[256,1024]{1,0:T(8,128)(2,1)S(1)}, bf16[256,1024]{1,0:T(8,128)(2,1)S(1)}, u32[]{:S(2)}, u32[]{:S(2)}) collective-permute-start(bf16[256,1024]{1,0:T(8,128)(2,1)S(1)} %get-tuple-element.66), channel_id=1, source_target_pairs={{0,16},{4,12},{8,24},{12,4},{16,0},{20,28},{24,8},{28,20},{1,17},{... | collective-permute-start | bytes 1572872 | tf_op jit(solution)/shard_map/ppermute | solution.py:34
  116.2 9.2 %collective-permute-start.32 = (bf16[128,1152]{1,0:T(8,128)(2,1)S(1)}, bf16[128,1152]{1,0:T(8,128)(2,1)S(1)}, u32[]{:S(2)}, u32[]{:S(2)}) collective-permute-start(bf16[128,1152]{1,0:T(8,128)(2,1)S(1)} %shard_map.168.refs_2_.refs_0_), channel_id=1, source_target_pairs={{0,4},{4,0},{8,12},{12,8},{16,20},{20,16},{24,28},{28,24},{1,5},{5... | collective-permute-start | bytes 884744 | tf_op jit(solution)/shard_map/ppermute | solution.py:34
  116.3 9.0 %collective-permute-start.23 = (bf16[64,1024]{1,0:T(8,128)(2,1)S(1)}, bf16[64,1024]{1,0:T(8,128)(2,1)S(1)}, u32[]{:S(2)}, u32[]{:S(2)}) collective-permute-start(bf16[64,1024]{1,0:T(8,128)(2,1)S(1)} %shard_map.165.refs_2_.refs_0_), channel_id=1, source_target_pairs={{0,8},{4,20},{8,0},{12,28},{16,24},{20,4},{24,16},{28,12},{1,9},{5... | collective-permute-start | bytes 393224 | tf_op jit(solution)/shard_map/ppermute | solution.py:34
  118.0 10.7 %collective-permute-start.31 = (bf16[64,1024]{1,0:T(8,128)(2,1)S(1)}, bf16[64,1024]{1,0:T(8,128)(2,1)S(1)}, u32[]{:S(2)}, u32[]{:S(2)}) collective-permute-start(bf16[64,1024]{1,0:T(8,128)(2,1)S(1)} %get-tuple-element.74), channel_id=1, source_target_pairs={{0,2},{1,3},{2,0},{3,1},{4,6},{5,7},{6,4},{7,5},{8,10},{9,11},{10,... | collective-permute-start | bytes 393224 | tf_op jit(solution)/shard_map/ppermute | solution.py:34
  118.9 10.6 %collective-permute-start.30 = (bf16[32,1024]{1,0:T(8,128)(2,1)S(1)}, bf16[32,1024]{1,0:T(8,128)(2,1)S(1)}, u32[]{:S(2)}, u32[]{:S(2)}) collective-permute-start(bf16[32,1024]{1,0:T(8,128)(2,1)S(1)} %get-tuple-element.73), channel_id=1, source_target_pairs={{0,2},{1,3},{2,0},{3,1},{4,6},{5,7},{6,4},{7,5},{8,10},{9,11},{10,... | collective-permute-start | bytes 196616 | tf_op jit(solution)/shard_map/ppermute | solution.py:34
  123.3 10.2 %collective-permute-start.29 = (bf16[128,1024]{1,0:T(8,128)(2,1)}, bf16[128,1024]{1,0:T(8,128)(2,1)}, u32[]{:S(2)}, u32[]{:S(2)}) collective-permute-start(bf16[128,1024]{1,0:T(8,128)(2,1)} %get-tuple-element.72), channel_id=1, source_target_pairs={{0,1},{1,0},{2,3},{3,2},{4,5},{5,4},{6,7},{7,6},{8,9},{9,8},{10,11... | collective-permute-start | bytes 786440 | tf_op jit(solution)/shard_map/ppermute | solution.py:34
  125.3 10.4 %collective-permute-start.28 = (bf16[128,1024]{1,0:T(8,128)(2,1)S(1)}, bf16[128,1024]{1,0:T(8,128)(2,1)}, u32[]{:S(2)}, u32[]{:S(2)}) collective-permute-start(bf16[128,1024]{1,0:T(8,128)(2,1)S(1)} %shard_map.170.refs_2_.refs_0_), channel_id=1, source_target_pairs={{0,4},{4,0},{8,12},{12,8},{16,20},{20,16},{24,28},{28,24},{1,5},{5... | collective-permute-start | bytes 786440 | tf_op jit(solution)/shard_map/ppermute | solution.py:34
  135.4 7.7 %collective-permute-start.33 = (bf16[64,1024]{1,0:T(8,128)(2,1)S(1)}, bf16[64,1024]{1,0:T(8,128)(2,1)S(1)}, u32[]{:S(2)}, u32[]{:S(2)}) collective-permute-start(bf16[64,1024]{1,0:T(8,128)(2,1)S(1)} %get-tuple-element.76), channel_id=1, source_target_pairs={{0,2},{1,3},{2,0},{3,1},{4,6},{5,7},{6,4},{7,5},{8,10},{9,11},{10,... | collective-permute-start | bytes 393224 | tf_op jit(solution)/shard_map/ppermute | solution.py:34
  (45 other events, 184.1 us)

commit v3 on v0

v3 whole, which is shorter than its diff:
```python
import functools

import jax
import jax.numpy as jnp
from jax import lax
from jax.experimental import pallas as pl
from jax.experimental.pallas import tpu as pltpu
from jax.sharding import PartitionSpec as P

BF = jnp.bfloat16
F32 = jnp.float32
ROOM = 48 * 1024 * 1024
VMEM = pltpu.VMEM


def inner(left, right):
    return lax.dot_general(
        left, right, (((0,), (0,)), ((), ())), preferred_element_type=F32
    )


def outer(left, right):
    return lax.dot_general(
        left, right, (((1,), (1,)), ((), ())), preferred_element_type=F32
    )


def times(left, right):
    return jnp.dot(left, right, preferred_element_type=F32)


def swap(value, axis, masks):
    count = lax.axis_size(axis)
    pairs = [(i, i ^ masks[i % len(masks)]) for i in range(count)]
    return lax.ppermute(value, axis, pairs)


def like(rows, columns, kind):
    return jax.ShapeDtypeStruct((rows, columns), kind)


def whole(array):
    return pl.BlockSpec(array.shape, lambda n, s: (0,) * len(array.shape))


def run(body, outs, ins, after, numbers, grid=1, in_specs=None, out_specs=None, scratch=()):
    count, late = 1 + len(ins), len(after)

    def kernel(*refs):
        body(*refs[:count], *refs[count + late :])

    in_specs = in_specs or [None] * len(ins)
    out_specs = out_specs or [None] * len(outs)
    return pl.pallas_call(
        kernel,
        out_shape=tuple(outs),
        grid_spec=pltpu.PrefetchScalarGridSpec(
            num_scalar_prefetch=1,
            grid=(grid,),
            in_specs=[s or whole(a) for s, a in zip(in_specs, ins)]
            + [pl.BlockSpec(memory_space=pl.ANY)] * late,
            out_specs=tuple(s or whole(a) for s, a in zip(out_specs, outs)),
            scratch_shapes=list(scratch),
        ),
        compiler_params=pltpu.CompilerParams(vmem_limit_bytes=ROOM),
        cost_estimate=pl.CostEstimate(flops=0, bytes_accessed=0, transcendentals=0),
    )(numbers, *ins, *after)


def sort_body(patch, part, own, numbers, grad, *blocks):
    size = own * part
    row = lax.broadcasted_iota(jnp.int32, (size, grad.shape[0]), 0)
    source = lax.broadcasted_iota(jnp.int32, (size, grad.shape[0]), 1)
    for m, block in enumerate(blocks):
        wanted = (row % part) * patch + numbers[m] * own + row // part
        block[...] = times((source == wanted).astype(BF), grad[...]).astype(BF)


def join_body(part, own, count, numbers, *refs):
    blocks, joined = refs[:-1], refs[-1]
    for m, block in enumerate(blocks):
        for j in range(own):
            start = pl.multiple_of((j * count + numbers[m]) * part, part)
            joined[pl.ds(start, part), :] = block[j * part : (j + 1) * part, :]


def id_of(ids, place):
    lane = lax.broadcasted_iota(jnp.int32, ids.shape, 1)
    return jnp.sum(jnp.where(lane == place, ids[...] + 1, 0), axis=1, keepdims=True) - 1


def vocab_line(numbers, first, count, height):
    lane = lax.broadcasted_iota(jnp.int32, (1, count * height), 1)
    line = lane % height
    for n in range(count):
        line = line + jnp.where(lane // height == n, numbers[first + n] * height, 0)
    return line


def hot(ids, line):
    return jnp.where(ids == line, 1.0, 0.0).astype(BF)


def forward_body(
    own, tp_count, share_count, height,
    numbers, ids_own, ids_other, out_own, out_other, in_grad, proj, emb, gain, up,
    slots, normed, scale, r_rows, h_part, slope, table_kept, table_sent,
):
    n = pl.program_id(0)
    patches = ids_own.shape[0]
    slot = proj.shape[0]
    vocab = emb.shape[0]

    @pl.when(n == 0)
    def _():
        hots = []
        line = lax.broadcasted_iota(jnp.int32, (1, vocab), 1)
        for side, (ids, out) in enumerate(((ids_own, out_own), (ids_other, out_other))):
            for j in range(own):
                first = (side * own + j) * patches
                slots[first : first + patches, :] = out[:, j * slot : (j + 1) * slot]
                hots.append(hot(id_of(ids, numbers[0] * own + j - 1), line))
        u_rows = times(slots[...], proj[...])
        u_rows = u_rows + times(jnp.concatenate(hots, axis=0), emb[...])
        factor = lax.rsqrt(jnp.mean(u_rows * u_rows, axis=1, keepdims=True) + 1e-05)
        value = u_rows * factor
        scale[...] = factor
        normed[...] = value.astype(BF)
        r_rows[...] = (value * gain[...]).astype(BF)

    a_rows = times(r_rows[...], up[...])
    sig = jax.nn.sigmoid(a_rows)
    h_part[...] = (a_rows * sig).astype(BF)
    slope[...] = (sig * (1.0 + a_rows * (1.0 - sig))).astype(BF)

    @pl.when(n == share_count - 1)
    def _():
        for first, target in ((tp_count, table_kept), (tp_count + share_count, table_sent)):
            line = vocab_line(numbers, first, share_count, height)
            total = None
            for j in range(own):
                picked = hot(id_of(ids_own, numbers[0] * own + j), line)
                term = inner(picked, in_grad[:, j * slot : (j + 1) * slot])
                total = term if total is None else total + term
            target[...] = total.astype(target.dtype)


def back_body(share_count, numbers, out_rows, slope, down, up, da, dr_part, dr_sent):
    n = pl.program_id(0)
    value = (outer(out_rows[...], down[...]) * slope[...].astype(F32)).astype(BF)
    da[...] = value
    term = outer(value, up[...])

    @pl.when(n == 0)
    def _():
        dr_part[...] = term

    @pl.when(n > 0)
    def _():
        dr_part[...] += term

    @pl.when(n == share_count - 1)
    def _():
        dr_sent[...] = dr_part[...].astype(BF)


def product_body(lefts, rights, unit, rows, seq_first, numbers, *refs):
    left, right = refs[:lefts], refs[lefts : lefts + rights]
    kept, sent, total = refs[lefts + rights :]
    n = pl.program_id(0)

    def piece(parts, i):
        if len(parts) > 1:
            return parts[i][...]
        return parts[0][i * rows : (i + 1) * rows, :]

    value = inner(piece(left, 0), piece(right, 0))
    value = value + inner(piece(left, 1), piece(right, 1))
    total[...] = value
    count = total.shape[0] // unit

    def put(target, places):
        for i, m in enumerate(places):
            start = pl.multiple_of(numbers[m] * unit, unit)
            block = total[pl.ds(start, unit), :]
            target[i * unit : (i + 1) * unit, :] = block.astype(target.dtype)

    if seq_first:
        reverse = sorted(range(count), key=lambda m: bin(m + count)[:2:-1])

        @pl.when(n < pl.num_programs(0) // 2)
        def _():
            put(kept, reverse)

        @pl.when(n >= pl.num_programs(0) // 2)
        def _():
            put(sent, reverse)

    else:
        ordered = sorted(range(count), key=lambda m: bin(m + count)[:2:-1])
        put(kept, ordered[: count // 2])
        put(sent, ordered[count // 2 :])


def norm_body(
    own, tp_count, share_count, height,
    numbers, part_own, part_other, more_own, more_other, normed, scale, gain, out_own,
    out_other, ids_own, ids_other, table_kept, table_more,
    du, kept, sent,
):
    patches = ids_own.shape[0]
    rows = part_own.shape[0]
    line = vocab_line(numbers, tp_count, share_count, height)
    gains = None
    table = None
    sides = (
        (part_own, more_own, out_own, ids_own),
        (part_other, more_other, out_other, ids_other),
    )
    for side, (part, more, out, ids) in enumerate(sides):
        at = slice(side * rows, (side + 1) * rows)
        dr = part[...] + more[...].astype(F32)
        unit = normed[at, :].astype(F32)
        term = jnp.sum(dr * unit, axis=0, keepdims=True)
        gains = term if gains is None else gains + term
        dn = dr * gain[...]
        mean = jnp.mean(dn * unit, axis=1, keepdims=True)
        value = (out[...].astype(F32) + scale[at, :] * (dn - unit * mean)).astype(BF)
        du[at, :] = value
        for j in range(own):
            picked = hot(id_of(ids, numbers[0] * own + j - 1), line)
            term = inner(picked, value[j * patches : (j + 1) * patches, :])
            table = term if table is None else table + term
    width = normed.shape[1]
    strip = width // (2 * share_count)
    lane = lax.broadcasted_iota(jnp.int32, (16, width), 1)
    row = lax.broadcasted_iota(jnp.int32, (16, width), 0)
    other = table_kept[...] + table_more[...].astype(F32)
    size = 2 * height + 16
    for n in range(share_count):
        target = kept if n < share_count // 2 else sent
        first = (n % (share_count // 2)) * size
        at = slice(n * height, (n + 1) * height)
        target[first : first + height, :] = other[at, :].astype(BF)
        target[first + height : first + 2 * height, :] = table[at, :].astype(BF)
        mine = (lane // strip == numbers[tp_count + n]) & (row == 0)
        target[first + 2 * height : first + size, :] = jnp.where(mine, gains, 0.0).astype(BF)


def spread_body(own, numbers, du, proj, out):
    patches = out.shape[0]
    slot = proj.shape[0]
    for j in range(own):
        value = outer(du[j * patches : (j + 1) * patches, :], proj[...])
        out[:, j * slot : (j + 1) * slot] = value.astype(BF)


def add_body(numbers, kept, arrived, keep, send):
    half = keep.shape[0]
    keep[...] = (kept[:half, :].astype(F32) + arrived[:half, :].astype(F32)).astype(keep.dtype)
    send[...] = (kept[half:, :].astype(F32) + arrived[half:, :].astype(F32)).astype(send.dtype)


def sum_body(numbers, kept, arrived, summed):
    summed[...] = (kept[...].astype(F32) + arrived[...].astype(F32)).astype(summed.dtype)


def turned_body(numbers, kept, arrived, summed):
    summed[...] = (kept[...].astype(F32) + arrived[...].astype(F32)).T


def stack_body(numbers, first, second, both):
    rows = first.shape[0]
    both[:rows, :] = first[...]
    both[rows:, :] = second[...]


def tables_body(numbers, first, second, place, glob, local, gain):
    half = first.shape[0]
    vocab = glob.shape[0]
    row = lax.broadcasted_iota(jnp.int32, (vocab, half), 0)
    for which, target in enumerate((glob, local)):
        total = None
        for side, value in enumerate((first, second)):
            line = place[which : which + 1, side * half : (side + 1) * half]
            term = times(hot(row, line), value[...])
            total = term if total is None else total + term
        target[...] = total
    mark = place[2:10, :].astype(F32).astype(BF)
    gains = times(mark[:, :half], first[...]) + times(mark[:, half:], second[...])
    gain[...] = gains[:1, :]


def on_device(
    byte_ids,
    global_out,
    global_in_grad,
    out_grad,
    proj_weight,
    emb_local,
    norm_gain,
    up_weight,
    down_weight,
):
    seq_count = lax.axis_size("seq")
    tp_count = lax.axis_size("tp")
    seq_place = lax.axis_index("seq")
    tp_place = lax.axis_index("tp")
    core = seq_place & 1
    chip = seq_place >> 1
    stages = seq_count.bit_length() - 2
    levels = tp_count.bit_length() - 1
    share_count = 1 << stages
    walks = (list(range(1, stages + 1)), list(range(stages, 0, -1)))
    patches, patch = byte_ids.shape
    slot, width = proj_weight.shape
    hidden = up_weight.shape[1]
    vocab = emb_local.shape[0]
    own = patch // tp_count
    part = patches // tp_count
    rows = own * patches
    height = vocab // seq_count
    chunk = hidden // seq_count

    def share_mask(number, walk):
        mask = 0
        for k in range(stages):
            if (number >> (stages - 1 - k)) & 1:
                mask |= 1 << (walk[k] - 1)
        return mask

    def shares_of(which):
        return [
            2 * (chip ^ jnp.where(which == 0, share_mask(n, walks[0]), share_mask(n, walks[1])))
            + which
            for n in range(share_count)
        ]

    shares = shares_of(core)
    others = shares_of(1 - core)
    near = [tp_place ^ m for m in range(tp_count)]
    numbers = jnp.stack(near + shares + others).astype(jnp.int32)
    call = functools.partial(run, numbers=numbers)

    def core_swap(value):
        return swap(value, "seq", (1,))

    def go(value, step):
        kind, k = step
        if kind == "seq":
            return swap(value, "seq", (1 << walks[0][k], 1 << walks[1][k]))
        return swap(value, "tp", (1 << k,))

    ids_other = core_swap(byte_ids)
    out_other = core_swap(global_out)
    blocks = call(
        functools.partial(sort_body, patch, part, own),
        [like(own * part, width, BF)] * tp_count,
        [out_grad],
        [],
    )
    blocks = [swap(b, "tp", (m,)) if m else b for m, b in enumerate(blocks)]

    by_share = pl.BlockSpec((2 * rows, chunk), lambda n, s: (0, n))
    up_spec = pl.BlockSpec((slot, chunk), lambda n, s: (0, s[tp_count + n]))
    down_spec = pl.BlockSpec((chunk, width), lambda n, s: (s[tp_count + n], 0))
    gain_line = norm_gain.reshape(1, width)
    slots, normed, scale, r_rows, h_rows, slope, glob_kept, glob_sent = call(
        functools.partial(forward_body, own, tp_count, share_count, height),
        [
            like(2 * rows, slot, BF),
            like(2 * rows, width, BF),
            like(2 * rows, 1, F32),
            like(2 * rows, width, BF),
            like(2 * rows, share_count * chunk, BF),
            like(2 * rows, share_count * chunk, BF),
            like(vocab // 2, width, F32),
            like(vocab // 2, width, BF),
        ],
        [
            byte_ids, ids_other, global_out, out_other, global_in_grad,
            proj_weight, emb_local, gain_line, up_weight,
        ],
        [blocks[0]],
        grid=share_count,
        in_specs=[None] * 8 + [up_spec],
        out_specs=[None] * 4 + [by_share, by_share, None, None],
    )
    glob_more = core_swap(glob_sent)

    (grad_own,) = call(
        functools.partial(join_body, part, own, tp_count),
        [like(rows, width, BF)],
        blocks,
        [r_rows],
    )
    grad_other = core_swap(grad_own)

    def back(grad, side, after):
        return call(
            functools.partial(back_body, share_count),
            [
                like(rows, share_count * chunk, BF),
                like(rows, width, F32),
                like(rows, width, BF),
            ],
            [grad, slope, down_weight, up_weight],
            after,
            grid=share_count,
            in_specs=[
                None,
                pl.BlockSpec((rows, chunk), lambda n, s: (side, n)),
                down_spec,
                up_spec,
            ],
            out_specs=[pl.BlockSpec((rows, chunk), lambda n, s: (0, n)), None, None],
        )

    def product(lefts, rights, share, seq_first, moving, after):
        unit = share // tp_count
        kind = BF if unit % 16 == 0 else F32
        columns = rights[0].shape[1]
        if moving and share % 128:
            lefts = [
                jnp.concatenate(
                    [lax.dynamic_slice_in_dim(x, s * share, share, 1) for s in shares], axis=1
                )
                for x in lefts
            ]
            moving = False

        def left_spec(array):
            if share % 128:
                return None
            if moving:
                return pl.BlockSpec((array.shape[0], share), lambda n, s: (0, s[tp_count + n]))
            return pl.BlockSpec((array.shape[0], share), lambda n, s: (0, n))

        grid = share_count
        if share % 128:
            return slow_product(lefts, rights, share, seq_first, after)
        half = share_count // 2
        if seq_first:
            out_specs = [
                pl.BlockSpec((share, columns), lambda n, s: (jnp.minimum(n, half - 1), 0)),
                pl.BlockSpec((share, columns), lambda n, s: (jnp.maximum(n - half, 0), 0)),
            ]
        else:
            out_specs = [pl.BlockSpec((share // 2, columns), lambda n, s: (n, 0))] * 2
        return call(
            functools.partial(
                product_body, len(lefts), len(rights), unit, rows, seq_first
            ),
            [like(share * share_count // 2, columns, kind)] * 2,
            [*lefts, *rights],
            after,
            grid=grid,
            in_specs=[left_spec(x) for x in lefts] + [None] * len(rights),
            out_specs=out_specs,
            scratch=[VMEM((share, columns), F32)],
        )

    def slow_product(lefts, rights, share, seq_first, after):
        left = jnp.concatenate(lefts, axis=0)
        right = jnp.concatenate(rights, axis=0)
        unit = share // tp_count
        value = inner(left, right).reshape(share_count, tp_count, unit, -1)
        value = jnp.stack(
            [lax.dynamic_index_in_dim(value, m, 1, keepdims=False) for m in near], axis=1
        )
        order = sorted(range(tp_count), key=lambda m: bin(m + tp_count)[:2:-1])
        value = jnp.stack([value[:, m] for m in order], axis=1)
        if not seq_first:
            value = value.reshape(share_count, 2, tp_count // 2, unit, -1).swapaxes(0, 1)
        value = value.reshape(2, share * share_count // 2, -1)
        value = value.astype(BF if unit % 16 == 0 else F32)
        return value[0], value[1]

    seq_steps = [("seq", k) for k in range(stages)]
    tp_steps = [("tp", k) for k in range(levels)]
    orders = {True: seq_steps + tp_steps, False: tp_steps[:1] + seq_steps + tp_steps[1:]}

    class Chain:
        def __init__(self, halves, seq_first, turned):
            self.kept, sent = halves
            self.steps, self.turned, self.at = orders[seq_first], turned, 0
            self.arrived = go(sent, self.steps[0])
            self.left = len(self.steps)

        def next(self, after):
            self.at += 1
            self.left -= 1
            rows, columns = self.kept.shape
            ins = [self.kept, self.arrived]
            if self.left:
                outs = [like(rows // 2, columns, self.kept.dtype)] * 2
                self.kept, sent = call(add_body, outs, ins, after)
                self.arrived = go(sent, self.steps[self.at])
            elif self.turned:
                (self.kept,) = call(turned_body, [like(columns, rows, F32)], ins, after)
            else:
                (self.kept,) = call(sum_body, [like(rows, columns, F32)], ins, after)
            return self.kept

    class Table:
        def __init__(self, kept, sent):
            self.kept, self.at = kept, 0
            self.plan = (
                [("half", s) for s in seq_steps]
                + [("sum", s) for s in tp_steps]
                + [("join", s) for s in reversed(seq_steps)]
                + [("join", None)]
            )
            self.left = len(self.plan) - 1
            self.arrived = go(sent, self.plan[0][1])

        def next(self, after):
            last, (kind, step) = self.plan[self.at][0], self.plan[self.at + 1]
            rows, columns = self.kept.shape
            ins = [self.kept, self.arrived]
            if last == "half" and kind == "half":
                self.kept, sent = call(add_body, [like(rows // 2, columns, BF)] * 2, ins, after)
            elif last == "join":
                (self.kept,) = call(stack_body, [like(2 * rows, columns, BF)], ins, after)
                sent = self.kept
            else:
                (self.kept,) = call(sum_body, [like(rows, columns, BF)], ins, after)
                sent = self.kept
            self.at += 1
            self.left -= 1
            self.arrived = core_swap(sent) if step is None else go(sent, step)
            return self.kept

    da_own, dr_own, dr_own_sent = back(grad_own, 0, [glob_kept])
    dr_other_more = core_swap(dr_own_sent)
    down = Chain(
        product([h_rows], [grad_own, grad_other], chunk, True, False, [da_own]), True, False
    )
    da_other, dr_other, dr_other_sent = back(grad_other, 1, [down.kept])
    dr_own_more = core_swap(dr_other_sent)
    up = Chain(
        product([da_own, da_other], [r_rows], chunk, False, False, [dr_other]), False, True
    )
    size = 2 * height + 16
    du_rows, kept, sent = call(
        functools.partial(norm_body, own, tp_count, share_count, height),
        [like(2 * rows, width, BF)] + [like(share_count // 2 * size, width, BF)] * 2,
        [
            dr_own, dr_other, dr_own_more, dr_other_more, normed, scale, gain_line, grad_own,
            grad_other, byte_ids, ids_other, glob_kept, glob_more,
        ],
        [up.kept],
    )
    table = Table(kept, sent)
    proj = Chain(
        product([du_rows], [slots], width // seq_count, True, True, [kept]), True, True
    )
    (glob_out_grad,) = call(
        functools.partial(spread_body, own),
        [like(patches, own * slot, BF)],
        [du_rows, proj_weight],
        [proj.kept],
        in_specs=[pl.BlockSpec((rows, width), lambda n, s: (0, 0)), None],
    )

    last = glob_out_grad
    queue = [
        down, table, proj, down, table, proj, up, table, down, proj, table, up, down,
        table, proj, up, table, up, table,
    ]
    for chain in queue + [table, proj, down, up] * 16:
        if chain.left:
            last = chain.next([last])

    all_numbers = jnp.stack(shares + others)
    inside = jnp.arange(size)[None, :]
    own_row = all_numbers[:, None] * height + inside
    place = jnp.stack(
        [
            jnp.where(inside < height, own_row, -1).reshape(-1),
            jnp.where(
                (inside >= height) & (inside < 2 * height), own_row - height, -1
            ).reshape(-1),
        ]
        + [jnp.broadcast_to(inside == 2 * height, own_row.shape).reshape(-1).astype(jnp.int32)] * 8
    ).astype(jnp.int32)
    emb_global_grad, emb_local_grad, gain_grad = call(
        tables_body,
        [like(vocab, width, F32), like(vocab, width, F32), like(1, width, F32)],
        [table.kept, table.arrived, place],
        [last],
    )
    return (
        glob_out_grad,
        emb_global_grad,
        emb_local_grad,
        gain_grad.reshape(width),
        proj.kept,
        up.kept,
        down.kept,
    )


def solution(mesh):
    placed = (
        P("seq", None),
        P("seq", "tp"),
        P("seq", "tp"),
        P(("seq", "tp"), None),
        P(),
        P(),
        P(),
        P(),
        P(),
    )
    return jax.shard_map(
        on_device,
        mesh=mesh,
        in_specs=placed,
        out_specs=(
            P("seq", "tp"),
            P(),
            P(),
            P(),
            P(None, ("seq", "tp")),
            P(None, ("seq", "tp")),
            P(("seq", "tp"), None),
        ),
        check_vma=False,
    )
```

time: 358 us -> 138 us (0.39)
  waiting for transfers between devices: 246 us -> 33.5 us
  Pallas kernels: 0 us -> 54.5 us
  blocking collectives: 41.2 us -> 0 us
  matrix products: 22.1 us -> 0 us
  starting transfers between devices: 11.5 us -> 32.2 us
  between operations: 15.8 us -> 1.03 us
    reduce_scatter x5 -> x0, waiting for transfers between devices: 157 us -> none  [the longest x1 54.6 us: on_device(): lax.psum_scatter(up_part.astype(jnp.bfloat16), 'seq', scatter_dimension=1...]
    psum x1 -> x0, waiting for transfers between devices: 75.7 us -> none  [on_device(): lax.psum((emb_global_part, emb_local_part, gain_part), ('seq', 'tp'))]
    pallas_call x0 -> x29, Pallas kernels: none -> 54.5 us  [run(): pl.pallas_call(kernel, out_shape=tuple(outs), grid_spec=pltpu.PrefetchSca...]
    psum x1 -> x0, blocking collectives: 41.2 us -> none  [on_device(): lax.psum((emb_global_part, emb_local_part, gain_part), ('seq', 'tp'))]
    ppermute x0 -> x28, waiting for transfers between devices: none -> 33.5 us  [swap(): return lax.ppermute(value, axis, pairs)]
    ppermute x0 -> x28, starting transfers between devices: none -> 32.2 us  [swap(): return lax.ppermute(value, axis, pairs)]
    dot_general x11 -> x0, matrix products: 22.1 us -> none  [the longest x5 14.5 us: inner(): lax.dot_general(left, right, (((0,), (0,)), ((), ())), preferred_element_...]
    all_to_all x2 -> x0, waiting for transfers between devices: 13.5 us -> none  [the longest x1 13.5 us: on_device(): lax.all_to_all(global_out, 'tp', split_axis=0, concat_axis=1, tiled=True)]
  transfers between devices with their start and end apart: 9 -> 28, of which waited for: 6 -> 8; matrix products, arithmetic and copies ran while one was open for 7% -> 2% of each run, Pallas kernels for 0% -> 34%
where the time goes in v3:
time: 138 us; the launch traced here: 136 us
  Pallas kernels  54.5 us (39%)
  waiting for transfers between devices  33.5 us (24%)
  starting transfers between devices  32.2 us (23%)
  local copies, waits for them, and re-layouts  14.5 us (11%)
    pallas_call x29, Pallas kernels, run(): pl.pallas_call(kernel, out_shape=tuple(outs), grid_spec=pltpu.PrefetchSca...  54.5 us
    ppermute x28, waiting for transfers between devices, swap(): return lax.ppermute(value, axis, pairs)  33.5 us
    ppermute x28, starting transfers between devices, swap(): return lax.ppermute(value, axis, pairs)  32.2 us
    unnamed x43, local copies, waits for them, and re-layouts  14 us
  transfers between devices with their start and end apart: 28, of which 8 were waited for; matrix products, arithmetic and copies ran while one was open for 2% of the time, Pallas kernels for 34%

profile of v3, /device:TPU:0, one launch (start us, length us, event | category | flops | bytes accessed | tf_op | source)
XLA Modules:
  0.0 135.8 jit_solution(5975954804776936180)
XLA Ops:
  3.3 2.7 %collective-permute-start = (bf16[64,1024]{1,0:T(8,128)(2,1)S(1)}, bf16[64,1024]{1,0:T(8,128)(2,1)S(1)}, u32[]{:S(2)}, u32[]{:S(2)}) collective-permute-start(bf16[64,1024]{1,0:T(8,128)(2,1)S(1)} %get-tuple-element.58), channel_id=1, source_target_pairs={{0,1},{1,0},{2,3},{3,2},{4,5},{5,4},{6,7},{7,6},{8,9},{9,8},{10,11... | collective-permute-start | bytes 393224 | tf_op jit(solution)/shard_map/ppermute | solution.py:35
  6.0 2.6 %collective-permute-start.1 = (bf16[64,1024]{1,0:T(8,128)(2,1)S(1)}, bf16[64,1024]{1,0:T(8,128)(2,1)S(1)}, u32[]{:S(2)}, u32[]{:S(2)}) collective-permute-start(bf16[64,1024]{1,0:T(8,128)(2,1)S(1)} %get-tuple-element.59), channel_id=1, source_target_pairs={{0,2},{1,3},{2,0},{3,1},{4,6},{5,7},{6,4},{7,5},{8,10},{9,11},{10,... | collective-permute-start | bytes 393224 | tf_op jit(solution)/shard_map/ppermute | solution.py:35
  14.5 8.9 %shard_map.145 = (bf16[512,1024]{1,0:T(8,128)(2,1)S(1)}, bf16[512,1024]{1,0:T(8,128)(2,1)S(1)}, f32[512,1]{1,0:T(8,128)S(1)}, bf16[512,1024]{1,0:T(8,128)(2,1)},...) custom-call(s32[12]{0:T(128)S(1)} %stack.73.refs_0_, ...), custom_call_target="tpu_custom_call" | custom-call | tf_op jit(solution)/shard_map/pallas_call | solution.py:54
  24.2 1.6 %copy-done.4 = bf16[512,1024]{1,0:T(8,128)(2,1)S(1)} copy-done((bf16[512,1024]{1,0:T(8,128)(2,1)S(1)}, bf16[512,1024]{1,0:T(8,128)(2,1)}, u32[]{:S(2)}) %copy-start.4) | copy-done | bytes 1048600
  27.8 5.9 %shard_map.147 = (bf16[256,1024]{1,0:T(8,128)(2,1)S(1)}, f32[256,1024]{1,0:T(8,128)S(1)}, bf16[256,1024]{1,0:T(8,128)(2,1)S(1)}) custom-call(s32[12]{0:T(128)S(1)} %stack.73.refs_0_, bf16[256,1024]{1,0:T(8,128)(2,1)S(1)} %shard_map.146.refs_1_.refs_2_.refs_8_, bf16[512,1024]{1,0:T(8,128)(2,1)S(1)} %copy-done.6, bf16[2048,1024]{1,0:T(8,128)(2,1)} %refs_3_.5, ...), custom_call_target="tpu_custom_call" | custom-call | tf_op jit(solution)/shard_map/pallas_call | solution.py:54
  33.8 3.6 %shard_map.148 = (bf16[512,1024]{1,0:T(8,128)(2,1)S(1)}, bf16[512,1024]{1,0:T(8,128)(2,1)}) custom-call(s32[12]{0:T(128)S(1)} %stack.73.refs_0_, bf16[512,1024]{1,0:T(8,128)(2,1)S(1)} %copy-done.10, bf16[256,1024]{1,0:T(8,128)(2,1)S(1)} %shard_map.146.refs_1_.refs_2_.refs_8_, bf16[256,1024]{1,0:T(8,128)(2,1)S(1)} %collective-permute-done.5.refs_3_.refs_1_.refs_9_, ...), custom_call_target="tpu_custom_call" | custom-call | tf_op jit(solution)/shard_map/pallas_call | solution.py:54
  37.4 1.7 %collective-permute-start.10 = (bf16[512,1024]{1,0:T(8,128)(2,1)}, bf16[512,1024]{1,0:T(8,128)(2,1)S(1)}, u32[]{:S(2)}, u32[]{:S(2)}) collective-permute-start(bf16[512,1024]{1,0:T(8,128)(2,1)} %get-tuple-element.81), channel_id=1, source_target_pairs={{0,8},{4,20},{8,0},{12,28},{16,24},{20,4},{24,16},{28,12},{1,9},{5... | collective-permute-start | bytes 3145736 | tf_op jit(solution)/shard_map/ppermute | solution.py:35
  39.2 6.7 %shard_map.149 = (bf16[256,1024]{1,0:T(8,128)(2,1)S(1)}, f32[256,1024]{1,0:T(8,128)S(1)}, bf16[256,1024]{1,0:T(8,128)(2,1)}) custom-call(s32[12]{0:T(128)S(1)} %stack.73.refs_0_, bf16[256,1024]{1,0:T(8,128)(2,1)S(1)} %collective-permute-done.5.refs_3_.refs_1_.refs_9_, bf16[512,1024]{1,0:T(8,128)(2,1)S(1)} %copy-done.7, bf16[2048,1024]{1,0:T(8,128)(2,1)} %refs_3_.5, ...), custom_call_target="tpu_custom_call" | custom-call | tf_op jit(solution)/shard_map/pallas_call | solution.py:54
  46.4 3.6 %shard_map.150 = (bf16[512,1024]{1,0:T(8,128)(2,1)S(1)}, bf16[512,1024]{1,0:T(8,128)(2,1)}) custom-call(s32[12]{0:T(128)S(1)} %stack.73.refs_0_, bf16[256,1024]{1,0:T(8,128)(2,1)S(1)} %get-tuple-element.66.refs_4_.refs_1_, bf16[256,1024]{1,0:T(8,128)(2,1)S(1)} %get-tuple-element.74.refs_2_, bf16[512,1024]{1,0:T(8,128)(2,1)S(1)} %copy-done.5, ...), custom_call_target="tpu_custom_call" | custom-call | tf_op jit(solution)/shard_map/pallas_call | solution.py:54
  51.8 3.8 %shard_map.151 = (bf16[512,1024]{1,0:T(8,128)(2,1)S(1)}, bf16[160,1024]{1,0:T(8,128)(2,1)S(1)}, bf16[160,1024]{1,0:T(8,128)(2,1)S(1)}) custom-call(s32[12]{0:T(128)S(1)} %stack.73.refs_0_, f32[256,1024]{1,0:T(8,128)S(1)} %get-tuple-element.64.refs_1_, f32[256,1024]{1,0:T(8,128)} %copy-done.3, bf16[256,1024]{1,0:T(8,128)(2,1)S(1)} %collective-permute-done.6.refs_3_, ...), custom_call_target="tpu_custom_call" | custom-call | tf_op jit(solution)/shard_map/pallas_call | solution.py:54
  55.6 2.4 %shard_map.152 = (bf16[256,1024]{1,0:T(8,128)(2,1)S(1)}, bf16[256,1024]{1,0:T(8,128)(2,1)S(1)}) custom-call(s32[12]{0:T(128)S(1)} %stack.73.refs_0_, bf16[512,1024]{1,0:T(8,128)(2,1)S(1)} %get-tuple-element.76.refs_1_, bf16[512,1024]{1,0:T(8,128)(2,1)S(1)} %get-tuple-element.77.refs_2_, bf16[160,1024]{1,0:T(8,128)(2,1)S(1)} %get-tuple-element.78.refs_3_.refs_1_), custom_call_target="tpu_custom_call" | custom-call | tf_op jit(solution)/shard_map/pallas_call | solution.py:54
  58.1 1.6 %collective-permute-start.13 = (bf16[256,1024]{1,0:T(8,128)(2,1)S(1)}, bf16[256,1024]{1,0:T(8,128)(2,1)S(1)}, u32[]{:S(2)}, u32[]{:S(2)}) collective-permute-start(bf16[256,1024]{1,0:T(8,128)(2,1)S(1)} %get-tuple-element.86), channel_id=1, source_target_pairs={{0,8},{4,20},{8,0},{12,28},{16,24},{20,4},{24,16},{28,12},{1,9},{5... | collective-permute-start | bytes 1572872 | tf_op jit(solution)/shard_map/ppermute | solution.py:35
  60.2 2.8 %shard_map.153.refs_3_ = bf16[128,2048]{1,0:T(8,128)(2,1)} custom-call(s32[12]{0:T(128)S(1)} %stack.73.refs_0_, bf16[512,1024]{1,0:T(8,128)(2,1)S(1)} %get-tuple-element.76.refs_1_, bf16[1024,1024]{1,0:T(8,128)(2,1)S(1)} %copy-done, bf16[256,1024]{1,0:T(8,128)(2,1)S(1)} %get-tuple-element.79.refs_3_.refs_1_), custom_call_target="tpu_custom_call" | custom-call | tf_op jit(solution)/shard_map/pallas_call | solution.py:54
  64.9 1.5 %collective-permute-start.12 = (bf16[256,1024]{1,0:T(8,128)(2,1)S(1)}, bf16[256,1024]{1,0:T(8,128)(2,1)S(1)}, u32[]{:S(2)}, u32[]{:S(2)}) collective-permute-start(bf16[256,1024]{1,0:T(8,128)(2,1)S(1)} %get-tuple-element.85), channel_id=1, source_target_pairs={{0,16},{4,12},{8,24},{12,4},{16,0},{20,28},{24,8},{28,20},{1,17},{... | collective-permute-start | bytes 1572872 | tf_op jit(solution)/shard_map/ppermute | solution.py:35
  66.4 8.0 %collective-permute-done.9.refs_2_ = bf16[160,1024]{1,0:T(8,128)(2,1)S(1)} collective-permute-done((bf16[160,1024]{1,0:T(8,128)(2,1)S(1)}, bf16[160,1024]{1,0:T(8,128)(2,1)S(1)}, u32[]{:S(2)}, u32[]{:S(2)}) %collective-permute-start.9) | collective-permute-done | bytes 327712 | tf_op jit(solution)/shard_map/ppermute | solution.py:35
  75.7 1.4 %collective-permute-start.16 = (bf16[128,1024]{1,0:T(8,128)(2,1)S(1)}, bf16[128,1024]{1,0:T(8,128)(2,1)S(1)}, u32[]{:S(2)}, u32[]{:S(2)}) collective-permute-start(bf16[128,1024]{1,0:T(8,128)(2,1)S(1)} %get-tuple-element.90), channel_id=1, source_target_pairs={{0,16},{4,12},{8,24},{12,4},{16,0},{20,28},{24,8},{28,20},{1,17},{... | collective-permute-start | bytes 786440 | tf_op jit(solution)/shard_map/ppermute | solution.py:35
  78.5 5.4 %collective-permute-done.11.refs_2_ = bf16[80,1024]{1,0:T(8,128)(2,1)S(1)} collective-permute-done((bf16[80,1024]{1,0:T(8,128)(2,1)S(1)}, bf16[80,1024]{1,0:T(8,128)(2,1)S(1)}, u32[]{:S(2)}, u32[]{:S(2)}) %collective-permute-start.11) | collective-permute-done | bytes 163872 | tf_op jit(solution)/shard_map/ppermute | solution.py:35
  85.9 2.0 %collective-permute-start.22 = (bf16[256,1024]{1,0:T(8,128)(2,1)S(1)}, bf16[256,1024]{1,0:T(8,128)(2,1)S(1)}, u32[]{:S(2)}, u32[]{:S(2)}) collective-permute-start(bf16[256,1024]{1,0:T(8,128)(2,1)S(1)} %get-tuple-element.98), channel_id=1, source_target_pairs={{0,8},{4,20},{8,0},{12,28},{16,24},{20,4},{24,16},{28,12},{1,9},{5... | collective-permute-start | bytes 1572872 | tf_op jit(solution)/shard_map/ppermute | solution.py:35
  87.9 1.3 collective-permute-start.14
  90.0 3.3 %collective-permute-done.14.refs_2_ = bf16[80,1024]{1,0:T(8,128)(2,1)S(1)} collective-permute-done((bf16[80,1024]{1,0:T(8,128)(2,1)S(1)}, bf16[80,1024]{1,0:T(8,128)(2,1)S(1)}, u32[]{:S(2)}, u32[]{:S(2)}) %collective-permute-start.14) | collective-permute-done | bytes 163872 | tf_op jit(solution)/shard_map/ppermute | solution.py:35
  93.9 5.3 %collective-permute-start.17 = (bf16[80,1024]{1,0:T(8,128)(2,1)S(1)}, bf16[80,1024]{1,0:T(8,128)(2,1)S(1)}, u32[]{:S(2)}, u32[]{:S(2)}) collective-permute-start(bf16[80,1024]{1,0:T(8,128)(2,1)S(1)} %shard_map.161.refs_3_.refs_1_), channel_id=1, source_target_pairs={{0,2},{1,3},{2,0},{3,1},{4,6},{5,7},{6,4},{7,5},{8,10},{9,11},{10,... | collective-permute-start | bytes 491528 | tf_op jit(solution)/shard_map/ppermute | solution.py:35
  99.2 1.6 %collective-permute-start.18 = (bf16[64,1024]{1,0:T(8,128)(2,1)S(1)}, bf16[64,1024]{1,0:T(8,128)(2,1)S(1)}, u32[]{:S(2)}, u32[]{:S(2)}) collective-permute-start(bf16[64,1024]{1,0:T(8,128)(2,1)S(1)} %get-tuple-element.93), channel_id=1, source_target_pairs={{0,1},{1,0},{2,3},{3,2},{4,5},{5,4},{6,7},{7,6},{8,9},{9,8},{10,11... | collective-permute-start | bytes 393224 | tf_op jit(solution)/shard_map/ppermute | solution.py:35
  101.4 3.8 %collective-permute-done.18.refs_2_ = bf16[64,1024]{1,0:T(8,128)(2,1)S(1)} collective-permute-done((bf16[64,1024]{1,0:T(8,128)(2,1)S(1)}, bf16[64,1024]{1,0:T(8,128)(2,1)S(1)}, u32[]{:S(2)}, u32[]{:S(2)}) %collective-permute-start.18) | collective-permute-done | bytes 131104 | tf_op jit(solution)/shard_map/ppermute | solution.py:35
  106.4 1.3 collective-permute-start.21
  108.4 3.9 %collective-permute-done.21.refs_2_ = bf16[64,1024]{1,0:T(8,128)(2,1)S(1)} collective-permute-done((bf16[64,1024]{1,0:T(8,128)(2,1)S(1)}, bf16[64,1024]{1,0:T(8,128)(2,1)S(1)}, u32[]{:S(2)}, u32[]{:S(2)}) %collective-permute-start.21) | collective-permute-done | bytes 131104 | tf_op jit(solution)/shard_map/ppermute | solution.py:35
  112.3 1.3 shard_map.166.refs_3_
  115.6 1.6 %collective-permute-start.24 = (bf16[128,1024]{1,0:T(8,128)(2,1)S(1)}, bf16[128,1024]{1,0:T(8,128)(2,1)S(1)}, u32[]{:S(2)}, u32[]{:S(2)}) collective-permute-start(bf16[128,1024]{1,0:T(8,128)(2,1)S(1)} %get-tuple-element.100), channel_id=1, source_target_pairs={{0,16},{4,12},{8,24},{12,4},{16,0},{20,28},{24,8},{28,20},{1,17},{... | collective-permute-start | bytes 786440 | tf_op jit(solution)/shard_map/ppermute | solution.py:35
  117.2 1.2 collective-permute-start.25
  118.6 3.8 %collective-permute-done.25.refs_2_ = bf16[32,1024]{1,0:T(8,128)(2,1)S(1)} collective-permute-done((bf16[32,1024]{1,0:T(8,128)(2,1)S(1)}, bf16[32,1024]{1,0:T(8,128)(2,1)S(1)}, u32[]{:S(2)}, u32[]{:S(2)}) %collective-permute-start.25) | collective-permute-done | bytes 65568 | tf_op jit(solution)/shard_map/ppermute | solution.py:35
  124.5 1.7 %collective-permute-start.27 = (bf16[64,1024]{1,0:T(8,128)(2,1)S(1)}, bf16[64,1024]{1,0:T(8,128)(2,1)S(1)}, u32[]{:S(2)}, u32[]{:S(2)}) collective-permute-start(bf16[64,1024]{1,0:T(8,128)(2,1)S(1)} %get-tuple-element.103), channel_id=1, source_target_pairs={{0,2},{1,3},{2,0},{3,1},{4,6},{5,7},{6,4},{7,5},{8,10},{9,11},{10,... | collective-permute-start | bytes 393224 | tf_op jit(solution)/shard_map/ppermute | solution.py:35
  127.4 3.9 %collective-permute-done.27.refs_2_ = bf16[64,1024]{1,0:T(8,128)(2,1)S(1)} collective-permute-done((bf16[64,1024]{1,0:T(8,128)(2,1)S(1)}, bf16[64,1024]{1,0:T(8,128)(2,1)S(1)}, u32[]{:S(2)}, u32[]{:S(2)}) %collective-permute-start.27) | collective-permute-done | bytes 131104 | tf_op jit(solution)/shard_map/ppermute | solution.py:35
  132.9 2.8 %shard_map.172 = (f32[256,1024]{1,0:T(8,128)}, f32[256,1024]{1,0:T(8,128)}, f32[1,1024]{1,0:T(1,128)}) custom-call(s32[12]{0:T(128)S(1)} %stack.73.refs_0_, bf16[320,1024]{1,0:T(8,128)(2,1)S(1)} %shard_map.170.refs_3_.refs_1_, bf16[320,1024]{1,0:T(8,128)(2,1)S(1)} %collective-permute-done.26.refs_2_, s32[10,640]{1,0:T(8,128)S(1)} %stack.75.refs_3_, ...), custom_call_target="tpu_custom_call" | custom-call | tf_op jit(solution)/shard_map/pallas_call | solution.py:54
  (107 shorter events, 31.4 us)
Async XLA Ops:
  0.6 10.1 %collective-permute-start.4 = (bf16[128,2048]{1,0:T(8,128)(2,1)}, bf16[128,2048]{1,0:T(8,128)(2,1)S(1)}, u32[]{:S(2)}, u32[]{:S(2)}) collective-permute-start(bf16[128,2048]{1,0:T(8,128)(2,1)} %refs_3_.3), channel_id=1, source_target_pairs={{0,4},{4,0},{8,12},{12,8},{16,20},{20,16},{24,28},{28,24},{1,5},{5... | collective-permute-start | bytes 1572872 | tf_op jit(solution)/shard_map/ppermute | solution.py:35
  3.3 20.8 %collective-permute-start = (bf16[64,1024]{1,0:T(8,128)(2,1)S(1)}, bf16[64,1024]{1,0:T(8,128)(2,1)S(1)}, u32[]{:S(2)}, u32[]{:S(2)}) collective-permute-start(bf16[64,1024]{1,0:T(8,128)(2,1)S(1)} %get-tuple-element.58), channel_id=1, source_target_pairs={{0,1},{1,0},{2,3},{3,2},{4,5},{5,4},{6,7},{7,6},{8,9},{9,8},{10,11... | collective-permute-start | bytes 393224 | tf_op jit(solution)/shard_map/ppermute | solution.py:35
  6.0 18.2 %collective-permute-start.1 = (bf16[64,1024]{1,0:T(8,128)(2,1)S(1)}, bf16[64,1024]{1,0:T(8,128)(2,1)S(1)}, u32[]{:S(2)}, u32[]{:S(2)}) collective-permute-start(bf16[64,1024]{1,0:T(8,128)(2,1)S(1)} %get-tuple-element.59), channel_id=1, source_target_pairs={{0,2},{1,3},{2,0},{3,1},{4,6},{5,7},{6,4},{7,5},{8,10},{9,11},{10,... | collective-permute-start | bytes 393224 | tf_op jit(solution)/shard_map/ppermute | solution.py:35
  8.6 15.6 %collective-permute-start.2 = (bf16[64,1024]{1,0:T(8,128)(2,1)S(1)}, bf16[64,1024]{1,0:T(8,128)(2,1)S(1)}, u32[]{:S(2)}, u32[]{:S(2)}) collective-permute-start(bf16[64,1024]{1,0:T(8,128)(2,1)S(1)} %get-tuple-element.60), channel_id=1, source_target_pairs={{0,3},{1,2},{2,1},{3,0},{4,7},{5,6},{6,5},{7,4},{8,11},{9,10},{10,... | collective-permute-start | bytes 393224 | tf_op jit(solution)/shard_map/ppermute | solution.py:35
  9.4 1.3 collective-permute-start.3
  26.4 7.4 %collective-permute-start.5 = (bf16[256,1024]{1,0:T(8,128)(2,1)S(1)}, bf16[256,1024]{1,0:T(8,128)(2,1)S(1)}, u32[]{:S(2)}, u32[]{:S(2)}) collective-permute-start(bf16[256,1024]{1,0:T(8,128)(2,1)S(1)} %shard_map.146.refs_1_.refs_2_.refs_8_), channel_id=1, source_target_pairs={{0,4},{4,0},{8,12},{12,8},{16,20},{20,16},{24,28},{28,24},{1,5},{5... | collective-permute-start | bytes 1572872 | tf_op jit(solution)/shard_map/ppermute | solution.py:35
  27.8 11.4 %copy-start.7 = (bf16[512,1024]{1,0:T(8,128)(2,1)S(1)}, bf16[512,1024]{1,0:T(8,128)(2,1)}, u32[]{:S(2)}) copy-start(bf16[512,1024]{1,0:T(8,128)(2,1)} %get-tuple-element.62.refs_2_) | copy-start | bytes 3145732
  37.4 25.6 %collective-permute-start.10 = (bf16[512,1024]{1,0:T(8,128)(2,1)}, bf16[512,1024]{1,0:T(8,128)(2,1)S(1)}, u32[]{:S(2)}, u32[]{:S(2)}) collective-permute-start(bf16[512,1024]{1,0:T(8,128)(2,1)} %get-tuple-element.81), channel_id=1, source_target_pairs={{0,8},{4,20},{8,0},{12,28},{16,24},{20,4},{24,16},{28,12},{1,9},{5... | collective-permute-start | bytes 3145736 | tf_op jit(solution)/shard_map/ppermute | solution.py:35
  39.1 12.6 %collective-permute-start.7 = (bf16[256,1024]{1,0:T(8,128)(2,1)S(1)}, bf16[256,1024]{1,0:T(8,128)(2,1)S(1)}, u32[]{:S(2)}, u32[]{:S(2)}) collective-permute-start(bf16[256,1024]{1,0:T(8,128)(2,1)S(1)} %get-tuple-element.70), channel_id=1, source_target_pairs={{0,4},{4,0},{8,12},{12,8},{16,20},{20,16},{24,28},{28,24},{1,5},{5... | collective-permute-start | bytes 1572872 | tf_op jit(solution)/shard_map/ppermute | solution.py:35
  39.2 12.5 %copy-start.17 = (f32[512,1]{1,0:T(8,128)S(1)}, f32[512,1]{1,0:T(8,128)}, u32[]{:S(2)}) copy-start(f32[512,1]{1,0:T(8,128)} %copy-done.16) | copy-start | bytes 6148
  39.2 12.5 %copy-start.19 = (f32[1024]{0:T(1024)S(1)}, f32[1024]{0:T(1024)}, u32[]{:S(2)}) copy-start(f32[1024]{0:T(1024)} %param.15) | copy-start | bytes 12292
  45.9 5.8 %collective-permute-start.6 = (bf16[256,1024]{1,0:T(8,128)(2,1)}, bf16[256,1024]{1,0:T(8,128)(2,1)S(1)}, u32[]{:S(2)}, u32[]{:S(2)}) collective-permute-start(bf16[256,1024]{1,0:T(8,128)(2,1)} %get-tuple-element.69), channel_id=1, source_target_pairs={{0,4},{4,0},{8,12},{12,8},{16,20},{20,16},{24,28},{28,24},{1,5},{5... | collective-permute-start | bytes 1572872 | tf_op jit(solution)/shard_map/ppermute | solution.py:35
  46.3 5.4 %collective-permute-start.8 = (bf16[128,1024]{1,0:T(8,128)(2,1)S(1)}, bf16[128,1024]{1,0:T(8,128)(2,1)S(1)}, u32[]{:S(2)}, u32[]{:S(2)}) collective-permute-start(bf16[128,1024]{1,0:T(8,128)(2,1)S(1)} %get-tuple-element.73), channel_id=1, source_target_pairs={{0,4},{4,0},{8,12},{12,8},{16,20},{20,16},{24,28},{28,24},{1,5},{5... | collective-permute-start | bytes 786440 | tf_op jit(solution)/shard_map/ppermute | solution.py:35
  51.0 34.1 %collective-permute-start.15 = (bf16[512,1024]{1,0:T(8,128)(2,1)}, bf16[512,1024]{1,0:T(8,128)(2,1)S(1)}, u32[]{:S(2)}, u32[]{:S(2)}) collective-permute-start(bf16[512,1024]{1,0:T(8,128)(2,1)} %get-tuple-element.89), channel_id=1, source_target_pairs={{0,1},{1,0},{2,3},{3,2},{4,5},{5,4},{6,7},{7,6},{8,9},{9,8},{10,11... | collective-permute-start | bytes 3145736 | tf_op jit(solution)/shard_map/ppermute | solution.py:35
  58.1 17.0 %collective-permute-start.13 = (bf16[256,1024]{1,0:T(8,128)(2,1)S(1)}, bf16[256,1024]{1,0:T(8,128)(2,1)S(1)}, u32[]{:S(2)}, u32[]{:S(2)}) collective-permute-start(bf16[256,1024]{1,0:T(8,128)(2,1)S(1)} %get-tuple-element.86), channel_id=1, source_target_pairs={{0,8},{4,20},{8,0},{12,28},{16,24},{20,4},{24,16},{28,12},{1,9},{5... | collective-permute-start | bytes 1572872 | tf_op jit(solution)/shard_map/ppermute | solution.py:35
  59.6 14.8 %collective-permute-start.9 = (bf16[160,1024]{1,0:T(8,128)(2,1)S(1)}, bf16[160,1024]{1,0:T(8,128)(2,1)S(1)}, u32[]{:S(2)}, u32[]{:S(2)}) collective-permute-start(bf16[160,1024]{1,0:T(8,128)(2,1)S(1)} %get-tuple-element.80), channel_id=1, source_target_pairs={{0,8},{4,20},{8,0},{12,28},{16,24},{20,4},{24,16},{28,12},{1,9},{5... | collective-permute-start | bytes 983048 | tf_op jit(solution)/shard_map/ppermute | solution.py:35
  63.0 22.1 %copy-start.2 = (bf16[512,1024]{1,0:T(8,128)(2,1)S(1)}, bf16[512,1024]{1,0:T(8,128)(2,1)}, u32[]{:S(2)}) copy-start(bf16[512,1024]{1,0:T(8,128)(2,1)} %copy-done.1) | copy-start | bytes 3145732
  64.9 12.9 %collective-permute-start.12 = (bf16[256,1024]{1,0:T(8,128)(2,1)S(1)}, bf16[256,1024]{1,0:T(8,128)(2,1)S(1)}, u32[]{:S(2)}, u32[]{:S(2)}) collective-permute-start(bf16[256,1024]{1,0:T(8,128)(2,1)S(1)} %get-tuple-element.85), channel_id=1, source_target_pairs={{0,16},{4,12},{8,24},{12,4},{16,0},{20,28},{24,8},{28,20},{1,17},{... | collective-permute-start | bytes 1572872 | tf_op jit(solution)/shard_map/ppermute | solution.py:35
  75.7 8.8 %collective-permute-start.16 = (bf16[128,1024]{1,0:T(8,128)(2,1)S(1)}, bf16[128,1024]{1,0:T(8,128)(2,1)S(1)}, u32[]{:S(2)}, u32[]{:S(2)}) collective-permute-start(bf16[128,1024]{1,0:T(8,128)(2,1)S(1)} %get-tuple-element.90), channel_id=1, source_target_pairs={{0,16},{4,12},{8,24},{12,4},{16,0},{20,28},{24,8},{28,20},{1,17},{... | collective-permute-start | bytes 786440 | tf_op jit(solution)/shard_map/ppermute | solution.py:35
  77.2 6.8 %collective-permute-start.11 = (bf16[80,1024]{1,0:T(8,128)(2,1)S(1)}, bf16[80,1024]{1,0:T(8,128)(2,1)S(1)}, u32[]{:S(2)}, u32[]{:S(2)}) collective-permute-start(bf16[80,1024]{1,0:T(8,128)(2,1)S(1)} %get-tuple-element.84), channel_id=1, source_target_pairs={{0,16},{4,12},{8,24},{12,4},{16,0},{20,28},{24,8},{28,20},{1,17},{... | collective-permute-start | bytes 491528 | tf_op jit(solution)/shard_map/ppermute | solution.py:35
  85.9 21.8 %collective-permute-start.22 = (bf16[256,1024]{1,0:T(8,128)(2,1)S(1)}, bf16[256,1024]{1,0:T(8,128)(2,1)S(1)}, u32[]{:S(2)}, u32[]{:S(2)}) collective-permute-start(bf16[256,1024]{1,0:T(8,128)(2,1)S(1)} %get-tuple-element.98), channel_id=1, source_target_pairs={{0,8},{4,20},{8,0},{12,28},{16,24},{20,4},{24,16},{28,12},{1,9},{5... | collective-permute-start | bytes 1572872 | tf_op jit(solution)/shard_map/ppermute | solution.py:35
  87.9 5.4 %collective-permute-start.14 = (bf16[80,1024]{1,0:T(8,128)(2,1)S(1)}, bf16[80,1024]{1,0:T(8,128)(2,1)S(1)}, u32[]{:S(2)}, u32[]{:S(2)}) collective-permute-start(bf16[80,1024]{1,0:T(8,128)(2,1)S(1)} %shard_map.158.refs_3_.refs_1_), channel_id=1, source_target_pairs={{0,1},{1,0},{2,3},{3,2},{4,5},{5,4},{6,7},{7,6},{8,9},{9,8},{10,11... | collective-permute-start | bytes 491528 | tf_op jit(solution)/shard_map/ppermute | solution.py:35
  89.3 11.5 %collective-permute-start.19 = (bf16[128,1024]{1,0:T(8,128)(2,1)S(1)}, bf16[128,1024]{1,0:T(8,128)(2,1)S(1)}, u32[]{:S(2)}, u32[]{:S(2)}) collective-permute-start(bf16[128,1024]{1,0:T(8,128)(2,1)S(1)} %get-tuple-element.94), channel_id=1, source_target_pairs={{0,1},{1,0},{2,3},{3,2},{4,5},{5,4},{6,7},{7,6},{8,9},{9,8},{10,11... | collective-permute-start | bytes 786440 | tf_op jit(solution)/shard_map/ppermute | solution.py:35
  93.9 11.8 %collective-permute-start.17 = (bf16[80,1024]{1,0:T(8,128)(2,1)S(1)}, bf16[80,1024]{1,0:T(8,128)(2,1)S(1)}, u32[]{:S(2)}, u32[]{:S(2)}) collective-permute-start(bf16[80,1024]{1,0:T(8,128)(2,1)S(1)} %shard_map.161.refs_3_.refs_1_), channel_id=1, source_target_pairs={{0,2},{1,3},{2,0},{3,1},{4,6},{5,7},{6,4},{7,5},{8,10},{9,11},{10,... | collective-permute-start | bytes 491528 | tf_op jit(solution)/shard_map/ppermute | solution.py:35
  99.2 6.0 %collective-permute-start.18 = (bf16[64,1024]{1,0:T(8,128)(2,1)S(1)}, bf16[64,1024]{1,0:T(8,128)(2,1)S(1)}, u32[]{:S(2)}, u32[]{:S(2)}) collective-permute-start(bf16[64,1024]{1,0:T(8,128)(2,1)S(1)} %get-tuple-element.93), channel_id=1, source_target_pairs={{0,1},{1,0},{2,3},{3,2},{4,5},{5,4},{6,7},{7,6},{8,9},{9,8},{10,11... | collective-permute-start | bytes 393224 | tf_op jit(solution)/shard_map/ppermute | solution.py:35
  106.3 7.3 %collective-permute-start.20 = (bf16[80,1024]{1,0:T(8,128)(2,1)S(1)}, bf16[80,1024]{1,0:T(8,128)(2,1)S(1)}, u32[]{:S(2)}, u32[]{:S(2)}) collective-permute-start(bf16[80,1024]{1,0:T(8,128)(2,1)S(1)} %shard_map.164.refs_3_.refs_1_), channel_id=1, source_target_pairs={{0,16},{4,12},{8,24},{12,4},{16,0},{20,28},{24,8},{28,20},{1,17},{... | collective-permute-start | bytes 491528 | tf_op jit(solution)/shard_map/ppermute | solution.py:35
  106.4 5.9 %collective-permute-start.21 = (bf16[64,1024]{1,0:T(8,128)(2,1)S(1)}, bf16[64,1024]{1,0:T(8,128)(2,1)S(1)}, u32[]{:S(2)}, u32[]{:S(2)}) collective-permute-start(bf16[64,1024]{1,0:T(8,128)(2,1)S(1)} %get-tuple-element.97), channel_id=1, source_target_pairs={{0,2},{1,3},{2,0},{3,1},{4,6},{5,7},{6,4},{7,5},{8,10},{9,11},{10,... | collective-permute-start | bytes 393224 | tf_op jit(solution)/shard_map/ppermute | solution.py:35
  115.1 8.6 %collective-permute-start.23 = (bf16[160,1024]{1,0:T(8,128)(2,1)S(1)}, bf16[160,1024]{1,0:T(8,128)(2,1)S(1)}, u32[]{:S(2)}, u32[]{:S(2)}) collective-permute-start(bf16[160,1024]{1,0:T(8,128)(2,1)S(1)} %shard_map.167.refs_3_.refs_1_), channel_id=1, source_target_pairs={{0,8},{4,20},{8,0},{12,28},{16,24},{20,4},{24,16},{28,12},{1,9},{5... | collective-permute-start | bytes 983048 | tf_op jit(solution)/shard_map/ppermute | solution.py:35
  115.6 7.5 %collective-permute-start.24 = (bf16[128,1024]{1,0:T(8,128)(2,1)S(1)}, bf16[128,1024]{1,0:T(8,128)(2,1)S(1)}, u32[]{:S(2)}, u32[]{:S(2)}) collective-permute-start(bf16[128,1024]{1,0:T(8,128)(2,1)S(1)} %get-tuple-element.100), channel_id=1, source_target_pairs={{0,16},{4,12},{8,24},{12,4},{16,0},{20,28},{24,8},{28,20},{1,17},{... | collective-permute-start | bytes 786440 | tf_op jit(solution)/shard_map/ppermute | solution.py:35
  117.2 5.2 %collective-permute-start.25 = (bf16[32,1024]{1,0:T(8,128)(2,1)S(1)}, bf16[32,1024]{1,0:T(8,128)(2,1)S(1)}, u32[]{:S(2)}, u32[]{:S(2)}) collective-permute-start(bf16[32,1024]{1,0:T(8,128)(2,1)S(1)} %get-tuple-element.101), channel_id=1, source_target_pairs={{0,2},{1,3},{2,0},{3,1},{4,6},{5,7},{6,4},{7,5},{8,10},{9,11},{10,... | collective-permute-start | bytes 196616 | tf_op jit(solution)/shard_map/ppermute | solution.py:35
  124.4 8.6 %collective-permute-start.26 = (bf16[320,1024]{1,0:T(8,128)(2,1)S(1)}, bf16[320,1024]{1,0:T(8,128)(2,1)S(1)}, u32[]{:S(2)}, u32[]{:S(2)}) collective-permute-start(bf16[320,1024]{1,0:T(8,128)(2,1)S(1)} %shard_map.170.refs_3_.refs_1_), channel_id=1, source_target_pairs={{0,4},{4,0},{8,12},{12,8},{16,20},{20,16},{24,28},{28,24},{1,5},{5... | collective-permute-start | bytes 1966088 | tf_op jit(solution)/shard_map/ppermute | solution.py:35
  124.5 6.8 %collective-permute-start.27 = (bf16[64,1024]{1,0:T(8,128)(2,1)S(1)}, bf16[64,1024]{1,0:T(8,128)(2,1)S(1)}, u32[]{:S(2)}, u32[]{:S(2)}) collective-permute-start(bf16[64,1024]{1,0:T(8,128)(2,1)S(1)} %get-tuple-element.103), channel_id=1, source_target_pairs={{0,2},{1,3},{2,0},{3,1},{4,6},{5,7},{6,4},{7,5},{8,10},{9,11},{10,... | collective-permute-start | bytes 393224 | tf_op jit(solution)/shard_map/ppermute | solution.py:35
  (16 other events, 41.3 us)
